TPU v7x, 128 devices: a whole 4x4x4 slice. The times are simulated.
128 devices in a mesh: seq: 8 (over z, core), head: 8 (over x_hi, y), batch: 2 (over x_lo).
Axes of the slice: x: 4 (x_hi: 2, x_lo: 2; x = x_hi * 2 + x_lo), y: 4, z: 4, core: 2. Of those that a mesh axis runs over, the one named last changes fastest.
Arguments:
- tokens: bfloat16 [16384, 2048], P(('batch', 'seq')), parts along dimension 0, may hold values from -256 to 256
- w_shared: bfloat16 [2048, 2048], P(None, 'head'), may hold values from -0.125 to 0.125
- w_value: bfloat16 [2048, 2048], P(None, 'head'), may hold values from -0.125 to 0.125
- w_output: bfloat16 [2048, 2048], P('head'), may hold values from -0.125 to 0.125
- doc_length: int32 [2], P('batch'), parts along dimension 0, may hold values from 2048 to 8192
Outputs:
- attended: bfloat16 [16384, 2048], P(('batch', 'seq'), 'head'), parts along dimension 0
There are 2 independent parts, one for each index of `batch`. A program takes and returns all parts, laid end to end along the dimension named above; an argument that names none is the same for every part. Nothing has to cross between parts.
All inputs are finite; a program needn't handle non-finite values.
Results may differ from a plain program's by a relative error of at most 0.018.
Values may be sent and summed in bfloat16 or wider, within the bound.
No kernel may reach another device: no remote copies, remote signals or barrier semaphores. Data moves between devices by JAX's collectives and lax.ppermute only.
A program may use at most 192 MiB of HBM per device.

v0:
```python
import math

import jax
import jax.numpy as jnp
from jax import lax
from jax.sharding import PartitionSpec as P

HEAD_DIM = 128


def body(tokens, w_shared, w_value, w_output, doc_length):
    row_count = tokens.shape[0]
    head_count = w_shared.shape[1] // HEAD_DIM
    shared = jnp.dot(tokens, w_shared, preferred_element_type=jnp.float32).astype(jnp.bfloat16)
    values = jnp.dot(tokens, w_value, preferred_element_type=jnp.float32).astype(jnp.bfloat16)
    doc_len = doc_length[0]
    seq_place = lax.axis_index("seq")
    own_start = seq_place * row_count

    def factors(key_rows):
        wide = key_rows.reshape(key_rows.shape[0], head_count, HEAD_DIM).astype(jnp.float32)
        return lax.rsqrt(jnp.mean(wide * wide, axis=-1) + 1e-06) / math.sqrt(HEAD_DIM)

    def gram_tiles(queries, key_rows):
        left = queries.reshape(queries.shape[0], head_count, HEAD_DIM)
        right = key_rows.reshape(key_rows.shape[0], head_count, HEAD_DIM)
        return jnp.einsum("qhd,khd->hqk", left, right, preferred_element_type=jnp.float32)

    def absorb(running, products, key_factor, key_values, query_first):
        row_peak, weight_sum, context_sum = running
        query_rows = products.shape[1]
        key_rows = key_values.shape[0]
        key_pos = jnp.arange(key_rows, dtype=jnp.int32)
        query_pos = query_first + jnp.arange(query_rows, dtype=jnp.int32)
        allowed = (key_pos[None, :] < doc_len) & (key_pos[None, :] != query_pos[:, None])
        scores = products * key_factor.T[:, None, :]
        scores = jnp.where(allowed[None, :, :], scores, -1e30)
        new_peak = jnp.maximum(row_peak, jnp.max(scores, axis=-1))
        unnorm = jnp.where(allowed[None, :, :], jnp.exp(scores - new_peak[:, :, None]), 0.0)
        rescale = jnp.exp(row_peak - new_peak)
        weight_sum = jnp.sum(unnorm, axis=-1)
        mixed_values = jnp.einsum(
            "hqk,khd->qhd",
            unnorm.astype(jnp.bfloat16),
            key_values.reshape(key_rows, head_count, HEAD_DIM),
            preferred_element_type=jnp.float32,
        )
        context3 = (
            context_sum.reshape(query_rows, head_count, HEAD_DIM) * rescale.T[:, :, None]
            + mixed_values
        )
        return (new_peak, weight_sum, context3.reshape(query_rows, head_count * HEAD_DIM))

    empty_state = (
        jnp.full((head_count, row_count), -1e30, jnp.float32),
        jnp.zeros((head_count, row_count), jnp.float32),
        jnp.zeros((row_count, head_count * HEAD_DIM), jnp.float32),
    )

    def unchanged(state):
        return state

    remote_keys = lax.all_gather(shared, "seq", axis=0, tiled=True)
    remote_values = lax.all_gather(values, "seq", axis=0, tiled=True)

    def tile_work(inner):
        return absorb(
            inner, gram_tiles(shared, remote_keys), factors(remote_keys), remote_values, own_start
        )

    active = (own_start < doc_len) & (jnp.int32(0) < doc_len)
    running = lax.cond(active, tile_work, unchanged, empty_state)
    row_peak, weight_sum, context_sum = running
    query_valid = own_start + jnp.arange(row_count, dtype=jnp.int32) < doc_len
    denom = jnp.where(weight_sum > 0.0, weight_sum, 1.0)
    context3 = context_sum.reshape(row_count, head_count, HEAD_DIM) / denom.T[:, :, None]
    context = jnp.where(
        query_valid[:, None], context3.reshape(row_count, head_count * HEAD_DIM), 0.0
    ).astype(jnp.bfloat16)
    projected = jnp.dot(context, w_output, preferred_element_type=jnp.float32)
    return lax.psum_scatter(projected.astype(jnp.bfloat16), "head", scatter_dimension=1, tiled=True)


def solution(mesh):
    placed = (
        P(("batch", "seq"), None),
        P(None, "head"),
        P(None, "head"),
        P("head", None),
        P("batch"),
    )
    return jax.shard_map(
        body, mesh=mesh, in_specs=placed, out_specs=P(("batch", "seq"), "head"), check_vma=False
    )
```

profile of v0, /device:TPU:0, one launch (start us, length us, event | category | flops | bytes accessed | tf_op | source)
XLA Modules:
  0.0 302.1 jit_solution(13223162531170430214)
XLA Ops:
  6.5 0.0 copy-start
  6.5 0.0 all-gather.3.cloned.1.call-start
  6.5 4.6 %convolution_convert_fusion.2 = bf16[1024,256]{1,0:T(8,128)(2,1)} fusion(bf16[1024,2048]{1,0:T(8,128)(2,1)} %param.7, bf16[2048,256]{1,0:T(8,128)(2,1)} %param.8), kind=kOutput, calls=%fused_computation.26 | convolution fusion | flops 1074003968 | bytes 5767168 | tf_op jit(solution)/shard_map/dot_general | solution.py:14
  11.2 0.0 copy-start.1
  11.2 0.0 all-gather.3.cloned.1.call-update
  11.2 0.0 all-gather.5.cloned.1.call-start
  11.2 4.6 %convolution_convert_fusion.1 = bf16[1024,256]{1,0:T(8,128)(2,1)} fusion(bf16[1024,2048]{1,0:T(8,128)(2,1)} %param.7, bf16[2048,256]{1,0:T(8,128)(2,1)} %param.9), kind=kOutput, calls=%fused_computation.25 | convolution fusion | flops 1074003968 | bytes 5767168 | tf_op jit(solution)/shard_map/dot_general | solution.py:15
  15.8 0.0 all-gather.5.cloned.1.call-update
  15.8 0.0 reduce-scatter.2.cloned.1.call-start
  16.5 29.6 %all-gather.3.cloned.1.call-done = bf16[8192,256]{1,0:T(8,128)(2,1)} async-done(((bf16[1024,256]{1,0:T(8,128)(2,1)}), bf16[8192,256]{1,0:T(8,128)(2,1)}) %all-gather.3.cloned.1.call-update) | async-done | bytes 4194320 | tf_op jit(solution)/shard_map/all_gather | solution.py:63
  46.1 33.9 %all-gather.5.cloned.1.call-done = bf16[8192,256]{1,0:T(8,128)(2,1)} async-done(((bf16[1024,256]{1,0:T(8,128)(2,1)}), bf16[8192,256]{1,0:T(8,128)(2,1)}) %all-gather.5.cloned.1.call-update) | async-done | bytes 4194320 | tf_op jit(solution)/shard_map/all_gather | solution.py:64
  80.0 0.0 copy-done.1
  80.0 128.9 %conditional.1 = (f32[2,1024]{1,0:T(2,128)S(1)}, f32[1024,256]{0,1:T(8,128)S(1)}) conditional(s32[]{:T(128)} %convert_element_type.21, () %tuple.13, (s32[]{:T(128)}, s32[]{:T(128)}, bf16[1024,256]{1,0:T(8,128)(2,1)S(1)}, bf16[8192,256]{1,0:T(8,128)(2,1)}, bf16[8192,256]{1,0:T(8,128)(2,1)}) %tuple.28), branch_computations={%region_0.0_spmd, %region_1.5_spmd} | conditional | flops 8831413248 | bytes 266428432 | solution.py:72
  80.0 6.9 %reshape.72 = bf16[8192,2,128]{2,1,0:T(2,128)(2,1)} reshape(bf16[8192,256]{1,0:T(8,128)(2,1)} %get-tuple-element.18) | data formatting | bytes 8388608 | tf_op jit(solution)/shard_map/cond/branch_1_fun/reshape | solution.py:26
  86.9 14.9 %multiply_reduce_fusion = f32[8192,2]{1,0:T(8,128)S(1)} fusion(bf16[8192,2,128]{2,1,0:T(2,128)(2,1)} %reshape.72), kind=kLoop, calls=%fused_computation.9 | loop fusion | flops 6275072 | bytes 4259840 | tf_op jit(solution)/shard_map/cond/branch_1_fun/reduce_sum | solution.py:22
  101.8 2.6 rsqrt_multiply_fusion
  104.4 2.8 copy.19
  107.2 0.7 iota_compare_fusion.1
  107.9 11.5 %fusion.5 = pred[1024,8192]{1,0:T(8,128)(4,1)} fusion(s32[1024]{0:T(1024)S(1)} %iota_add_fusion, pred[8192]{0:T(1024)(128)(4,1)S(1)} %iota_compare_fusion.1), kind=kLoop, calls=%fused_computation.7 | loop fusion | flops 16777216 | bytes 8400896 | tf_op jit(solution)/shard_map/cond/branch_1_fun/and | solution.py:35
  119.4 28.5 %fusion = (f32[2,1024]{1,0:T(2,128)S(1)}, f32[2,1024,8192]{2,1,0:T(8,128)}) fusion(f32[2,8192]{1,0:T(2,128)S(1)} %bitcast.48, pred[1024,8192]{1,0:T(8,128)(4,1)} %fusion.5, bf16[8192,256]{1,0:T(8,128)(2,1)} %get-tuple-element.18, bf16[1024,256]{1,0:T(8,128)(2,1)S(1)} %get-tuple-element.17), kind=kOutput, calls=%fused_computation.2 | convolution fusion | flops 4345296896 | bytes 80289792 | tf_op jit(solution)/shard_map/cond/branch_1_fun/qhd,khd->hqk/dot_general | solution.py:27
  147.9 6.4 %copy.16 = bf16[8192,256]{0,1:T(8,128)(2,1)} copy(bf16[8192,256]{1,0:T(8,128)(2,1)} %get-tuple-element.38) | data formatting | bytes 8388608 | tf_op jit(solution)/shard_map
  154.4 30.0 %fusion.13 = f32[1024,2,128]{0,2,1:T(8,128)S(1)} fusion(bf16[8192,2,128]{0,2,1:T(8,128)(2,1)} %bitcast.46, f32[2,1024,8192]{2,1,0:T(8,128)} %get-tuple-element.42, f32[2,1024]{1,0:T(2,128)S(1)} %get-tuple-element.40, f32[2,8192]{1,0:T(2,128)S(1)} %bitcast.49, pred[1024,8192]{1,0:T(8,128)(4,1)} %fusion.5, f32[1024,2]{0,1:T(2,128)S(1)} %get-tuple-element.39), kind=kOutput, calls=%fused_computation.15 | convolution fusion | flops 4379115520 | bytes 80822272 | tf_op jit(solution)/shard_map/cond/branch_1_fun/hqk,khd->qhd/dot_general | solution.py:42
  184.4 24.2 %fusion.2 = f32[2,1024]{1,0:T(2,128)S(1)} fusion(f32[2,1024,8192]{2,1,0:T(8,128)} %get-tuple-element.42, f32[2,1024]{1,0:T(2,128)S(1)} %get-tuple-element.40, f32[2,8192]{1,0:T(2,128)S(1)} %bitcast.50, pred[1024,8192]{1,0:T(8,128)(4,1)} %fusion.5), kind=kLoop, calls=%fused_computation.4 | loop fusion | flops 83884032 | bytes 75579392 | tf_op jit(solution)/shard_map/cond/branch_1_fun/reduce_sum | solution.py:41
  208.9 0.1 fusion.21
  209.1 0.0 copy-done
  209.1 3.3 %convolution_convert_fusion = bf16[1024,2048]{1,0:T(8,128)(2,1)} fusion(bf16[1024,256]{0,1:T(8,128)(2,1)S(1)} %fusion.21, bf16[256,2048]{1,0:T(8,128)(2,1)S(1)} %copy-done), kind=kOutput, calls=%fused_computation.24 | convolution fusion | flops 1075838976 | bytes 5767168 | tf_op jit(solution)/shard_map/dot_general | solution.py:80
  212.3 0.0 reduce-scatter.2.cloned.1.call-update
  212.3 83.3 %reduce-scatter.2.cloned.1.call-done = bf16[1024,256]{1,0:T(8,128)(2,1)} async-done(((bf16[1024,2048]{1,0:T(8,128)(2,1)}), bf16[1024,256]{1,0:T(8,128)(2,1)}) %reduce-scatter.2.cloned.1.call-update) | async-done | bytes 524304 | tf_op jit(solution)/shard_map/reduce_scatter | solution.py:81
  (4 shorter events, 0.0 us)
Async XLA Ops:
  6.5 202.5 %copy-start = (bf16[256,2048]{1,0:T(8,128)(2,1)S(1)}, bf16[256,2048]{1,0:T(8,128)(2,1)}, u32[]{:S(2)}) copy-start(bf16[256,2048]{1,0:T(8,128)(2,1)} %param.10) | copy-start | bytes 3145732
  6.5 39.6 %all-gather.3.cloned.1.call-start = ((), (), s32[]{:S(2)}) async-start(), calls=%async_computation.1 | async-start | bytes 4718592 | tf_op jit(solution)/shard_map/all_gather | solution.py:63
  11.2 68.9 %copy-start.1 = (bf16[1024,256]{1,0:T(8,128)(2,1)S(1)}, bf16[1024,256]{1,0:T(8,128)(2,1)}, u32[]{:S(2)}) copy-start(bf16[1024,256]{1,0:T(8,128)(2,1)} %convolution_convert_fusion.2) | copy-start | bytes 1572868
  11.2 68.8 %all-gather.5.cloned.1.call-start = ((), (), s32[]{:S(2)}) async-start(), calls=%async_computation.2 | async-start | bytes 4718592 | tf_op jit(solution)/shard_map/all_gather | solution.py:64
  15.8 279.8 %reduce-scatter.2.cloned.1.call-start = ((), (), s32[]{:S(2)}) async-start(), calls=%async_computation.3 | async-start | bytes 4718592 | tf_op jit(solution)/shard_map/reduce_scatter | solution.py:81
Sparse Core Ops, SparseCore 0:
  11.3 34.7 all-gather.2
  47.9 32.1 all-gather.4
  212.5 83.1 reduce-scatter.1
where the time goes:
time: 303 us; the launch traced here: 302 us
  waiting for transfers between devices  147 us (49%)
  matrix products  71 us (23%)
  other arithmetic  54 us (18%)
  local copies, waits for them, and re-layouts  16.2 us (5%)
  between operations  13.8 us (5%)
    reduce_scatter x1, waiting for transfers between devices, body(): lax.psum_scatter(projected.astype(jnp.bfloat16), 'head', scatter_dimensio...  83.3 us
    all_gather x1, waiting for transfers between devices, body(): remote_values = lax.all_gather(values, 'seq', axis=0, tiled=True)  33.9 us
    dot_general x1, matrix products, absorb(): jnp.einsum('hqk,khd->qhd', unnorm.astype(jnp.bfloat16), key_values.reshap...  30 us
    all_gather x1, waiting for transfers between devices, body(): remote_keys = lax.all_gather(shared, 'seq', axis=0, tiled=True)  29.6 us
    dot_general x1, matrix products, gram_tiles(): jnp.einsum('qhd,khd->hqk', left, right, preferred_element_type=jnp.float32)  28.5 us
    reduce_sum x1, other arithmetic, absorb(): weight_sum = jnp.sum(unnorm, axis=-1)  24.2 us
    reduce_sum x1, other arithmetic, factors(): jnp.mean(wide * wide, axis=-1) + 1e-06  14.9 us
    and x1, other arithmetic, absorb(): (key_pos[None, :] < doc_len) & (key_pos[None, :] != query_pos[:, None])  11.5 us
  transfers between devices with their start and end apart: 3, of which 3 were waited for; matrix products, arithmetic and copies ran while one was open for 2% of the time, Pallas kernels for 0%

commit v1 on v0

v1 whole, which is shorter than its diff:
```python
import functools
import math

import jax
import jax.numpy as jnp
from jax import lax
from jax.experimental import pallas as pl
from jax.experimental.pallas import tpu as pltpu
from jax.sharding import PartitionSpec as P

HEAD_DIM = 128
LOG2E = 1.4426950408889634
NORM_LIMIT = 60.0
NT = (((1,), (1,)), ((), ()))
VMEM = 56 * 2**20


def project_kernel(head_ref, x_ref, ws_ref, wv_ref, out_ref, w_scr):
    @pl.when(pl.program_id(0) == 0)
    def _():
        w_scr[:, :HEAD_DIM] = ws_ref[...]
        w_scr[:, HEAD_DIM:] = wv_ref[...]

    out_ref[...] = jnp.dot(
        x_ref[...], w_scr[...], preferred_element_type=jnp.float32
    ).astype(out_ref.dtype)


def project(tokens, w_shared, w_value, head, name):
    rows, width = tokens.shape
    step = 256
    weight = pl.BlockSpec((width, HEAD_DIM), lambda i, h: (0, h[0]))
    return pl.pallas_call(
        project_kernel,
        grid_spec=pltpu.PrefetchScalarGridSpec(
            num_scalar_prefetch=1,
            grid=(rows // step,),
            in_specs=[pl.BlockSpec((step, width), lambda i, h: (i, 0)), weight, weight],
            out_specs=pl.BlockSpec((step, 2 * HEAD_DIM), lambda i, h: (i, 0)),
            scratch_shapes=[pltpu.VMEM((width, 2 * HEAD_DIM), jnp.bfloat16)],
        ),
        out_shape=jax.ShapeDtypeStruct((rows, 2 * HEAD_DIM), jnp.bfloat16),
        compiler_params=pltpu.CompilerParams(vmem_limit_bytes=VMEM),
        cost_estimate=pl.CostEstimate(
            flops=2 * rows * width * 256, bytes_accessed=6 * 2**20, transcendentals=0
        ),
        name=name,
    )(head.reshape(1), tokens, w_shared, w_value)


def attend_kernel(count, first, last, scal_ref, *refs):
    own_ref, peer_ref = refs[:2]
    kv_refs = refs[2 : 2 + count]
    refs = refs[2 + count :]
    acc_in = None
    if not first:
        acc_in, refs = refs[0], refs[1:]
    if first:
        out_ref, norm_ref, q_scr, f_scr, v_scr = refs
        acc = out_ref
    elif last:
        out_ref, q_scr, f_scr, v_scr, acc = refs
    else:
        out_ref, q_scr, f_scr, v_scr = refs
        acc = out_ref
    step = pl.program_id(0)
    doc_len = scal_ref[0]
    rows = own_ref.shape[0]
    tile = 512

    @pl.when(step == 0)
    def _():
        q_scr[...] = own_ref[:, :HEAD_DIM]
        largest = None
        for at, kv_ref in enumerate(kv_refs):
            wide = kv_ref[:, :HEAD_DIM].astype(jnp.float32)
            square = wide * wide
            high = square.astype(jnp.bfloat16)
            low = (square - high.astype(jnp.float32)).astype(jnp.bfloat16)
            ones = jnp.ones((8, HEAD_DIM), jnp.bfloat16)
            total = lax.dot_general(ones, high, NT, preferred_element_type=jnp.float32)
            total += lax.dot_general(ones, low, NT, preferred_element_type=jnp.float32)
            f_scr[at] = lax.rsqrt(total / HEAD_DIM + 1e-06) * (LOG2E / math.sqrt(HEAD_DIM))
            if first:
                top = jnp.max(total)
                largest = top if largest is None else jnp.maximum(largest, top)
            place = lax.broadcasted_iota(jnp.int32, (rows, HEAD_DIM), 0) + scal_ref[4 + at]
            valid = place < doc_len
            v_scr[at, :, :HEAD_DIM] = jnp.where(
                valid, kv_ref[:, HEAD_DIM:].astype(jnp.float32), 0.0
            ).astype(jnp.bfloat16)
            v_scr[at, :, HEAD_DIM:] = jnp.where(valid, 1.0, 0.0).astype(jnp.bfloat16)
        if first:
            norm_ref[0, 0] = largest

    @pl.when(step == 1)
    def _():
        q_scr[...] = peer_ref[:, :HEAD_DIM]

    query_start = scal_ref[2 + step]
    if first:
        acc[...] = jnp.zeros_like(acc)
    else:
        acc[...] = acc_in[...]
    for at, kv_ref in enumerate(kv_refs):

        @pl.when((query_start < doc_len) & (scal_ref[4 + at] < doc_len))
        def _(at=at, kv_ref=kv_ref):
            queries = q_scr[...]
            total = acc[...]
            for cut in range(rows // tile):
                keys = slice(cut * tile, (cut + 1) * tile)
                scores = lax.dot_general(
                    queries, kv_ref[keys, :HEAD_DIM], NT, preferred_element_type=jnp.float32
                )
                weights = jnp.exp2(scores * f_scr[at, 0:1, keys])
                if first:
                    apart = jnp.where(step == at, cut * tile, 4 * rows)
                    weights = jnp.where(
                        lax.broadcasted_iota(jnp.int32, weights.shape, 0)
                        == lax.broadcasted_iota(jnp.int32, weights.shape, 1) + apart,
                        0.0,
                        weights,
                    )
                total += jnp.dot(
                    weights.astype(jnp.bfloat16),
                    v_scr[at, keys, :],
                    preferred_element_type=jnp.float32,
                )
            acc[...] = total

    if last:
        total = acc[...]
        inside = (
            lax.broadcasted_iota(jnp.int32, (rows, HEAD_DIM), 0) + query_start < doc_len
        )
        mixed = jnp.where(inside, total[:, :HEAD_DIM] / total[:, HEAD_DIM:], 0.0)
        out_ref[...] = mixed.astype(out_ref.dtype).reshape(out_ref.shape)


def attend(scalars, own, peer, blocks, state, last, name):
    rows = own.shape[0]
    count = len(blocks)
    first = state is None
    whole = pl.BlockSpec((rows, 2 * HEAD_DIM), lambda i, s: (0, 0))
    sums = pl.BlockSpec((rows, 2 * HEAD_DIM), lambda i, s: (i, 0))
    out_shape = jax.ShapeDtypeStruct((2 * rows, 2 * HEAD_DIM), jnp.float32)
    out_specs = sums
    scratch = [
        pltpu.VMEM((rows, HEAD_DIM), jnp.bfloat16),
        pltpu.VMEM((count, 8, rows), jnp.float32),
        pltpu.VMEM((count, rows, 2 * HEAD_DIM), jnp.bfloat16),
    ]
    if first:
        out_shape = (out_shape, jax.ShapeDtypeStruct((1, 1), jnp.float32))
        out_specs = (sums, pl.BlockSpec(memory_space=pltpu.SMEM))
    if last:
        out_shape = jax.ShapeDtypeStruct((8, 2, rows // 8, HEAD_DIM), jnp.bfloat16)
        out_specs = pl.BlockSpec(
            (8, 1, rows // 8, HEAD_DIM),
            lambda i, s: (0, jnp.where(i == 0, s[1], 1 - s[1]), 0, 0),
        )
        scratch.append(pltpu.VMEM((rows, 2 * HEAD_DIM), jnp.float32))
    return pl.pallas_call(
        functools.partial(attend_kernel, count, first, last),
        grid_spec=pltpu.PrefetchScalarGridSpec(
            num_scalar_prefetch=1,
            grid=(2,),
            in_specs=[whole] * (2 + count) + ([] if first else [sums]),
            out_specs=out_specs,
            scratch_shapes=scratch,
        ),
        out_shape=out_shape,
        compiler_params=pltpu.CompilerParams(vmem_limit_bytes=VMEM),
        cost_estimate=pl.CostEstimate(
            flops=8 * 2 * rows * rows * count * HEAD_DIM,
            bytes_accessed=8 * 2**20,
            transcendentals=0,
        ),
        name=name,
    )(scalars, own, peer, *blocks, *([] if first else [state]))


def attend_with_peak(doc_len, core, own_starts, own, peer, blocks, starts):
    rows = own.shape[0]
    queries = jnp.concatenate([own[:, :HEAD_DIM], peer[:, :HEAD_DIM]])
    here = jnp.arange(rows, dtype=jnp.int32)
    query_pos = jnp.concatenate([own_starts[0] + here, own_starts[1] + here])

    def absorb(running, block):
        key_values, start = block
        peak, weight_sum, total = running
        keys, values = key_values[:, :HEAD_DIM], key_values[:, HEAD_DIM:]
        wide = keys.astype(jnp.float32)
        factor = lax.rsqrt(jnp.mean(wide * wide, axis=-1) + 1e-06) / math.sqrt(HEAD_DIM)
        key_pos = start + here
        allowed = (key_pos[None, :] < doc_len) & (key_pos[None, :] != query_pos[:, None])
        scores = jnp.dot(queries, keys.T, preferred_element_type=jnp.float32) * factor[None, :]
        scores = jnp.where(allowed, scores, -1e30)
        new_peak = jnp.maximum(peak, jnp.max(scores, axis=-1))
        weights = jnp.where(allowed, jnp.exp(scores - new_peak[:, None]), 0.0)
        rescale = jnp.exp(peak - new_peak)
        mixed = jnp.dot(weights.astype(jnp.bfloat16), values, preferred_element_type=jnp.float32)
        return (
            new_peak,
            weight_sum * rescale + jnp.sum(weights, axis=-1),
            total * rescale[:, None] + mixed,
        ), None

    empty = (
        jnp.full((2 * rows,), -1e30, jnp.float32),
        jnp.zeros((2 * rows,), jnp.float32),
        jnp.zeros((2 * rows, HEAD_DIM), jnp.float32),
    )
    (_, weight_sum, total), _ = lax.scan(absorb, empty, (jnp.stack(blocks), jnp.stack(starts)))
    denom = jnp.where(weight_sum > 0.0, weight_sum, 1.0)
    mixed = jnp.where((query_pos < doc_len)[:, None], total / denom[:, None], 0.0)
    mixed = mixed.astype(jnp.bfloat16).reshape(2, 8, rows // 8, HEAD_DIM)
    mixed = jnp.where(core == 0, mixed, mixed[::-1])
    return mixed.transpose(1, 0, 2, 3)


def output_kernel(scal_ref, near_ref, far_ref, w_near_ref, w_far_ref, out_ref):
    def side(ctx_ref, w_ref):
        left = jnp.concatenate([ctx_ref[g, 0] for g in range(4)], axis=1)
        return jnp.dot(left, w_ref[...], preferred_element_type=jnp.float32)

    total = side(near_ref, w_near_ref) + side(far_ref, w_far_ref)
    out_ref[0] = total.astype(out_ref.dtype)


def output_part(scalars, context, w_near, w_far, dtype, name):
    rows = context.shape[2]
    width = w_near.shape[1]
    ctx = (4, 1, rows, HEAD_DIM)
    return pl.pallas_call(
        output_kernel,
        grid_spec=pltpu.PrefetchScalarGridSpec(
            num_scalar_prefetch=1,
            grid=(width // 256,),
            in_specs=[
                pl.BlockSpec(ctx, lambda i, s: (s[0], s[1], 0, 0)),
                pl.BlockSpec(ctx, lambda i, s: (1 - s[0], s[1], 0, 0)),
                pl.BlockSpec((4 * HEAD_DIM, 256), lambda i, s: (0, i)),
                pl.BlockSpec((4 * HEAD_DIM, 256), lambda i, s: (0, i)),
            ],
            out_specs=pl.BlockSpec((1, rows, 256), lambda i, s: (i, 0, 0)),
        ),
        out_shape=jax.ShapeDtypeStruct((width // 256, rows, 256), dtype),
        compiler_params=pltpu.CompilerParams(vmem_limit_bytes=VMEM),
        cost_estimate=pl.CostEstimate(
            flops=2 * rows * width * 1024, bytes_accessed=5 * 2**20, transcendentals=0
        ),
        name=name,
    )(scalars, context, context, w_near, w_far)


def body(tokens, w_shared, w_value, w_output, doc_length):
    rows = tokens.shape[0]
    doc_len = doc_length[0]
    seq = lax.axis_index("seq")
    core = lax.rem(seq, 2)
    z = lax.div(seq, 2)
    x_hi = lax.div(lax.axis_index("head"), 4)

    def swap(array):
        return lax.ppermute(array, "seq", [(i, i ^ 1) for i in range(8)])

    def along_z(array, by):
        return lax.ppermute(array, "seq", [(i, (i + 2 * by) % 8) for i in range(8)])

    y_groups = [[0, 1, 2, 3], [4, 5, 6, 7]]
    w_own = lax.dynamic_slice_in_dim(w_output, core * HEAD_DIM, HEAD_DIM, 0)
    w_other = lax.ppermute(
        w_own,
        ("head", "batch"),
        [(h * 2 + b, (h ^ 4) * 2 + (1 - b)) for h in range(8) for b in range(2)],
    )
    w_near = lax.all_gather(w_own, "head", axis=0, axis_index_groups=y_groups, tiled=True)
    w_far = lax.all_gather(w_other, "head", axis=0, axis_index_groups=y_groups, tiled=True)

    given = project(tokens, w_shared, w_value, 1 - core, "project_given")
    peer = swap(given)
    own = project(tokens, w_shared, w_value, core, "project_own")

    own_left, peer_right = along_z(own, 1), along_z(peer, -1)
    peer_left, own_right = along_z(peer, 1), along_z(own, -1)
    own_far, peer_far = along_z(own_left, 1), along_z(peer_right, -1)

    def start_of(by, other):
        place = lax.rem(z + by, 4) * 2
        return (place + (1 - core if other else core)) * rows

    def scalars(*starts):
        return jnp.stack([doc_len, core, start_of(0, False), start_of(0, True), *starts])

    here = (start_of(0, False), start_of(0, True))
    near = (start_of(3, False), start_of(1, True), start_of(3, True), start_of(1, False))
    far = (start_of(2, False), start_of(2, True))
    state, norm = attend(scalars(*here), own, peer, (own, peer), None, False, "attend_here")
    near_blocks = (own_left, peer_right, peer_left, own_right)
    state = attend(scalars(*near), own, peer, near_blocks, state, False, "attend_near")
    context = attend(scalars(*far), own, peer, (own_far, peer_far), state, True, "attend_far")
    context = lax.cond(
        norm[0, 0] <= NORM_LIMIT**2,
        lambda: context,
        lambda: attend_with_peak(
            doc_len,
            core,
            here,
            own,
            peer,
            (own, peer, *near_blocks, own_far, peer_far),
            (*here, *near, *far),
        ),
    )
    context = lax.all_to_all(context, "head", 0, 0, tiled=True)
    given_part = output_part(
        jnp.stack([x_hi, 1 - core]), context, w_near, w_far, jnp.bfloat16, "output_given"
    )
    swapped = swap(given_part)
    own_part = output_part(
        jnp.stack([x_hi, core]), context, w_near, w_far, jnp.float32, "output_own"
    )
    result = (own_part + swapped.astype(jnp.float32)).astype(jnp.bfloat16)
    result = lax.all_to_all(result, "head", 0, 0, tiled=True)
    return result.reshape(rows, result.shape[-1])


def solution(mesh):
    placed = (
        P(("batch", "seq"), None),
        P(None, "head"),
        P(None, "head"),
        P("head", None),
        P("batch"),
    )
    return jax.shard_map(
        body, mesh=mesh, in_specs=placed, out_specs=P(("batch", "seq"), "head"), check_vma=False
    )
```

time: 303 us -> 285 us (0.941)
  waiting for transfers between devices: 147 us -> 29.8 us
  Pallas kernels: 0 us -> 57.6 us
  matrix products: 71 us -> 52.3 us
  starting transfers between devices: 0.09 us -> 18.6 us
  other arithmetic: 54 us -> 70.7 us
  blocking collectives: 0 us -> 15 us
  local copies, waits for them, and re-layouts: 16.2 us -> 25 us
    reduce_scatter x1 -> x0, waiting for transfers between devices: 83.3 us -> none  [body(): lax.psum_scatter(projected.astype(jnp.bfloat16), 'head', scatter_dimensio...]
    all_gather x2, waiting for transfers between devices: 63.5 us -> 0.01 us  [the longest x1 0.01 us: body(): lax.all_gather(w_own, 'head', axis=0, axis_index_groups=y_groups, tiled=T...]
    pallas_call x0 -> x7, Pallas kernels: none -> 57.6 us  [the longest x3 33.2 us: attend(): pl.pallas_call(functools.partial(attend_kernel, count, first, last), grid...]
    ppermute x0 -> x9, waiting for transfers between devices: none -> 19.4 us  [the longest x1 12.1 us: body(): lax.ppermute(w_own, ('head', 'batch'), [(h * 2 + b, (h ^ 4) * 2 + (1 - b)...]
    dot_general x5 -> x16, matrix products: 71 us -> 52.3 us  [the longest x8 36.3 us: absorb(): jnp.dot(queries, keys.T, preferred_element_type=jnp.float32)]
    all_to_all x0 -> x1, blocking collectives: none -> 15 us  [body(): result = lax.all_to_all(result, 'head', 0, 0, tiled=True)]
    reduce_sum x2 -> x16, other arithmetic: 39.1 us -> 52.2 us  [the longest x8 50.5 us: absorb(): jnp.sum(weights, axis=-1)]
    ppermute x0 -> x9, starting transfers between devices: none -> 12.8 us  [the longest x6 9.87 us: along_z(): return lax.ppermute(array, 'seq', [(i, (i + 2 * by) % 8) for i in range(8)])]
  transfers between devices with their start and end apart: 3 -> 12, of which waited for: 3 -> 4; matrix products, arithmetic and copies ran while one was open for 2% -> 49% of each run, Pallas kernels for 0% -> 18%
where the time goes in v1:
time: 285 us; the launch traced here: 284 us
  other arithmetic  70.7 us (25%)
  Pallas kernels  57.6 us (20%)
  matrix products  52.3 us (18%)
  waiting for transfers between devices  29.8 us (10%)
  local copies, waits for them, and re-layouts  25 us (9%)
  starting transfers between devices  18.6 us (7%)
  blocking collectives  15 us (5%)
  between operations  14.7 us (5%)
    reduce_sum x8, other arithmetic, absorb(): jnp.sum(weights, axis=-1)  50.5 us
    dot_general x8, matrix products, absorb(): jnp.dot(queries, keys.T, preferred_element_type=jnp.float32)  36.3 us
    pallas_call x3, Pallas kernels, attend(): pl.pallas_call(functools.partial(attend_kernel, count, first, last), grid...  33.2 us
    dot_general x8, matrix products, absorb(): jnp.dot(weights.astype(jnp.bfloat16), values, preferred_element_type=jnp....  16 us
    all_to_all x1, blocking collectives, body(): result = lax.all_to_all(result, 'head', 0, 0, tiled=True)  15 us
    pallas_call x2, Pallas kernels, output_part(): pl.pallas_call(output_kernel, grid_spec=pltpu.PrefetchScalarGridSpec(num_...  14.7 us
    ppermute x1, waiting for transfers between devices, body(): lax.ppermute(w_own, ('head', 'batch'), [(h * 2 + b, (h ^ 4) * 2 + (1 - b)...  12.1 us
    all_to_all x1, waiting for transfers between devices, body(): context = lax.all_to_all(context, 'head', 0, 0, tiled=True)  10.4 us
  transfers between devices with their start and end apart: 12, of which 4 were waited for; matrix products, arithmetic and copies ran while one was open for 49% of the time, Pallas kernels for 18%

profile of v1, /device:TPU:0, one launch (start us, length us, event | category | flops | bytes accessed | tf_op | source)
XLA Modules:
  0.0 284.4 jit_solution(12472939629588686675)
XLA Ops:
  6.5 1.2 copy-done
  8.7 2.9 %collective-permute-start.7 = (bf16[128,2048]{1,0:T(8,128)(2,1)}, bf16[128,2048]{1,0:T(8,128)(2,1)S(1)}, u32[]{:S(2)}, u32[]{:S(2)}) collective-permute-start(bf16[128,2048]{1,0:T(8,128)(2,1)} %constant_dynamic-slice_fusion), channel_id=1, source_target_pairs={{0,9},{1,8},{2,11},{3,10},{4,13},{5,12},{6,15},{7,14},{8,1},{9,0},... | collective-permute-start | bytes 1572872 | tf_op jit(solution)/shard_map/ppermute | solution.py:274
  11.6 12.1 %collective-permute-done.7 = bf16[128,2048]{1,0:T(8,128)(2,1)S(1)} collective-permute-done((bf16[128,2048]{1,0:T(8,128)(2,1)}, bf16[128,2048]{1,0:T(8,128)(2,1)S(1)}, u32[]{:S(2)}, u32[]{:S(2)}) %collective-permute-start.7) | collective-permute-done | bytes 524320 | tf_op jit(solution)/shard_map/ppermute | solution.py:274
  24.6 5.2 %project_given.1 = bf16[1024,256]{1,0:T(8,128)(2,1)} custom-call(s32[1]{0:T(128)} %bitcast.23.head_ref, bf16[1024,2048]{1,0:T(8,128)(2,1)} %x_ref.3, bf16[2048,256]{1,0:T(8,128)(2,1)} %ws_ref.3, bf16[2048,256]{1,0:T(8,128)(2,1)} %wv_ref.3), custom_call_target="tpu_custom_call" | custom-call | flops 1073741824 | bytes 6291456 | tf_op jit(solution)/shard_map/project_given/pallas_call | solution.py:33
  29.8 4.4 %project_own.1.refs_0_.refs_2_ = bf16[1024,256]{1,0:T(8,128)(2,1)S(1)} custom-call(s32[1]{0:T(128)} %bitcast.20.head_ref, bf16[1024,2048]{1,0:T(8,128)(2,1)} %x_ref.3, bf16[2048,256]{1,0:T(8,128)(2,1)} %ws_ref.3, bf16[2048,256]{1,0:T(8,128)(2,1)} %wv_ref.3), custom_call_target="tpu_custom_call" | custom-call | flops 1073741824 | bytes 6291456 | tf_op jit(solution)/shard_map/project_own/pallas_call | solution.py:33
  34.2 2.2 collective-permute-start.1
  36.4 2.2 collective-permute-start.2
  38.6 1.9 collective-permute-start.4
  43.2 8.1 %attend_here.1 = (f32[2048,256]{1,0:T(8,128)}, f32[1,1]{1,0:T(1,128)}) custom-call(s32[6]{0:T(128)} %stack.115.scal_ref, bf16[1024,256]{1,0:T(8,128)(2,1)S(1)} %project_own.1.refs_0_.refs_2_, bf16[1024,256]{1,0:T(8,128)(2,1)S(1)} %collective-permute-done.refs_1_.refs_3_, bf16[1024,256]{1,0:T(8,128)(2,1)S(1)} %project_own.1.refs_0_.refs_2_, ...), custom_call_target="tpu_custom_call" | custom-call | flops 4294967296 | bytes 8388608 | tf_op jit(solution)/shard_map/attend_here/pallas_call | solution.py:164
  52.0 3.4 %collective-permute-start.6 = (bf16[1024,256]{1,0:T(8,128)(2,1)S(1)}, bf16[1024,256]{1,0:T(8,128)(2,1)S(1)}, u32[]{:S(2)}, u32[]{:S(2)}) collective-permute-start(bf16[1024,256]{1,0:T(8,128)(2,1)S(1)} %collective-permute-done.2.refs_3_), channel_id=1, source_target_pairs={{0,96},{16,112},{32,0},{48,16},{64,32},{80,48},{96,64},{112,80},{1... | collective-permute-start | bytes 1572872 | tf_op jit(solution)/shard_map/ppermute | solution.py:270
  55.4 7.0 %collective-permute-done.4.refs_5_ = bf16[1024,256]{1,0:T(8,128)(2,1)} collective-permute-done((bf16[1024,256]{1,0:T(8,128)(2,1)S(1)}, bf16[1024,256]{1,0:T(8,128)(2,1)}, u32[]{:S(2)}, u32[]{:S(2)}) %collective-permute-start.4) | collective-permute-done | bytes 524320 | tf_op jit(solution)/shard_map/ppermute | solution.py:270
  62.6 15.8 %attend_near.1.refs_4_ = f32[2048,256]{1,0:T(8,128)} custom-call(s32[8]{0:T(128)} %stack.123.scal_ref, bf16[1024,256]{1,0:T(8,128)(2,1)S(1)} %project_own.1.refs_0_.refs_2_, bf16[1024,256]{1,0:T(8,128)(2,1)S(1)} %collective-permute-done.refs_1_.refs_3_, bf16[1024,256]{1,0:T(8,128)(2,1)S(1)} %collective-permute-done.1.refs_2_, ...), custom_call_target="tpu_custom_call" | custom-call | flops 8589934592 | bytes 8388608 | tf_op jit(solution)/shard_map/attend_near/pallas_call | solution.py:164
  78.4 9.3 %attend_far.1 = bf16[8,2,128,128]{3,2,1,0:T(8,128)(2,1)} custom-call(s32[6]{0:T(128)} %stack.118.scal_ref, bf16[1024,256]{1,0:T(8,128)(2,1)S(1)} %project_own.1.refs_0_.refs_2_, bf16[1024,256]{1,0:T(8,128)(2,1)S(1)} %collective-permute-done.refs_1_.refs_3_, bf16[1024,256]{1,0:T(8,128)(2,1)S(1)} %collective-permute-done.5.refs_2_, ...), custom_call_target="tpu_custom_call" | custom-call | flops 4294967296 | bytes 8388608 | tf_op jit(solution)/shard_map/attend_far/pallas_call | solution.py:164
  87.8 138.9 %conditional.1 = (bf16[8,2,128,128]{3,2,0,1:T(8,128)(2,1)S(1)}) conditional(s32[]{:T(128)} %bitcast.24, (s32[]{:T(128)}, s32[]{:T(128)}, s32[]{:T(128)}, s32[1]{0:T(128)}, bf16[1024,256]{1,0:T(8,128)(2,1)S(1)}, /*index=5*/bf16[1024,256]{1,0:T(8,128)(2,1)S(1)}, bf16[1024,256]{1,0:T(8,128)(2,1)S(1)}, bf16[1024,256]{1,0:T(8,128)(2,1)S(1)}, ...), branch_computations={%region_0.6_spmd, %region_6.7_spmd} | conditional | flops 1104309248 | bytes 59743596 | solution.py:304
  90.2 1.9 copy-done.2
  92.3 132.8 %while.14 = (s32[]{:T(128)}, f32[2048]{0:T(1024)S(1)}, f32[2048]{0:T(1024)S(1)}, f32[2048,128]{1,0:T(8,128)S(1)}, s32[8]{0:T(128)S(1)}, /*index=5*/s32[]{:T(128)...) while((s32[]{:T(128)}, f32[2048]{0:T(1024)S(1)}, ...), condition=%wide.region_5.5_spmd.clone, body=%wide.region_1.4_spmd.clone.sunk | while | flops 1102199808 | bytes 29797524 | solution.py:215
  94.2 1.2 broadcast_compare_fusion.3
  96.0 4.5 %fusion.26 = (f32[2048]{0:T(1024)S(1)}, f32[1024,2048]{1,0:T(8,128)}) fusion(f32[1024]{0:T(1024)S(1)} %rsqrt_multiply_fusion.2, s32[2048]{0:T(1024)S(1)} %get-tuple-element.276, s32[1024]{0:T(1024)S(1)} %iota_add_fusion.4, pred[1024]{0:T(1024)(128)(4,1)S(1)} %broadcast_compare_fusion.3, bf16[2048,128]{1,0:T(8,128)(2,1)S(1)} %get-tuple-element.278, ...), kind=kOutput, calls=%fused_computation.4.clone.1 | convolution fusion | flops 547354624 | bytes 9200640 | tf_op jit(solution)/shard_map/cond/branch_0_fun/while/body/eval_jaxpr/dot_general | solution.py:198
  100.6 6.3 %fusion.27 = (f32[2048]{0:T(1024)S(1)}, bf16[2048,1024]{0,1:T(8,128)(2,1)S(1)}) fusion(f32[2048]{0:T(1024)S(1)} %select_maximum_fusion.2, f32[1024,2048]{1,0:T(8,128)} %get-tuple-element.243, f32[1024]{0:T(1024)S(1)} %rsqrt_multiply_fusion.2, s32[2048]{0:T(1024)S(1)} %get-tuple-element.276, s32[1024]{0:T(1024)S(1)} %iota_add_fusion.4, ...), kind=kLoop, calls=%fused_computation.42.clone.1 | loop fusion | flops 16775168 | bytes 12616704 | tf_op jit(solution)/shard_map/cond/branch_0_fun/while/body/eval_jaxpr/reduce_sum | solution.py:206
  106.9 2.0 fusion.29
  110.8 1.2 broadcast_compare_fusion.3
  112.6 4.5 %fusion.26 = (f32[2048]{0:T(1024)S(1)}, f32[1024,2048]{1,0:T(8,128)}) fusion(f32[1024]{0:T(1024)S(1)} %rsqrt_multiply_fusion.2, s32[2048]{0:T(1024)S(1)} %get-tuple-element.276, s32[1024]{0:T(1024)S(1)} %iota_add_fusion.4, pred[1024]{0:T(1024)(128)(4,1)S(1)} %broadcast_compare_fusion.3, bf16[2048,128]{1,0:T(8,128)(2,1)S(1)} %get-tuple-element.278, ...), kind=kOutput, calls=%fused_computation.4.clone.1 | convolution fusion | flops 547354624 | bytes 9200640 | tf_op jit(solution)/shard_map/cond/branch_0_fun/while/body/eval_jaxpr/dot_general | solution.py:198
  117.2 6.3 %fusion.27 = (f32[2048]{0:T(1024)S(1)}, bf16[2048,1024]{0,1:T(8,128)(2,1)S(1)}) fusion(f32[2048]{0:T(1024)S(1)} %select_maximum_fusion.2, f32[1024,2048]{1,0:T(8,128)} %get-tuple-element.243, f32[1024]{0:T(1024)S(1)} %rsqrt_multiply_fusion.2, s32[2048]{0:T(1024)S(1)} %get-tuple-element.276, s32[1024]{0:T(1024)S(1)} %iota_add_fusion.4, ...), kind=kLoop, calls=%fused_computation.42.clone.1 | loop fusion | flops 16775168 | bytes 12616704 | tf_op jit(solution)/shard_map/cond/branch_0_fun/while/body/eval_jaxpr/reduce_sum | solution.py:206
  123.5 2.0 fusion.29
  129.2 4.5 %fusion.26 = (f32[2048]{0:T(1024)S(1)}, f32[1024,2048]{1,0:T(8,128)}) fusion(f32[1024]{0:T(1024)S(1)} %rsqrt_multiply_fusion.2, s32[2048]{0:T(1024)S(1)} %get-tuple-element.276, s32[1024]{0:T(1024)S(1)} %iota_add_fusion.4, pred[1024]{0:T(1024)(128)(4,1)S(1)} %broadcast_compare_fusion.3, bf16[2048,128]{1,0:T(8,128)(2,1)S(1)} %get-tuple-element.278, ...), kind=kOutput, calls=%fused_computation.4.clone.1 | convolution fusion | flops 547354624 | bytes 9200640 | tf_op jit(solution)/shard_map/cond/branch_0_fun/while/body/eval_jaxpr/dot_general | solution.py:198
  133.8 6.3 %fusion.27 = (f32[2048]{0:T(1024)S(1)}, bf16[2048,1024]{0,1:T(8,128)(2,1)S(1)}) fusion(f32[2048]{0:T(1024)S(1)} %select_maximum_fusion.2, f32[1024,2048]{1,0:T(8,128)} %get-tuple-element.243, f32[1024]{0:T(1024)S(1)} %rsqrt_multiply_fusion.2, s32[2048]{0:T(1024)S(1)} %get-tuple-element.276, s32[1024]{0:T(1024)S(1)} %iota_add_fusion.4, ...), kind=kLoop, calls=%fused_computation.42.clone.1 | loop fusion | flops 16775168 | bytes 12616704 | tf_op jit(solution)/shard_map/cond/branch_0_fun/while/body/eval_jaxpr/reduce_sum | solution.py:206
  140.1 2.0 fusion.29
  145.8 4.5 %fusion.26 = (f32[2048]{0:T(1024)S(1)}, f32[1024,2048]{1,0:T(8,128)}) fusion(f32[1024]{0:T(1024)S(1)} %rsqrt_multiply_fusion.2, s32[2048]{0:T(1024)S(1)} %get-tuple-element.276, s32[1024]{0:T(1024)S(1)} %iota_add_fusion.4, pred[1024]{0:T(1024)(128)(4,1)S(1)} %broadcast_compare_fusion.3, bf16[2048,128]{1,0:T(8,128)(2,1)S(1)} %get-tuple-element.278, ...), kind=kOutput, calls=%fused_computation.4.clone.1 | convolution fusion | flops 547354624 | bytes 9200640 | tf_op jit(solution)/shard_map/cond/branch_0_fun/while/body/eval_jaxpr/dot_general | solution.py:198
  150.4 6.3 %fusion.27 = (f32[2048]{0:T(1024)S(1)}, bf16[2048,1024]{0,1:T(8,128)(2,1)S(1)}) fusion(f32[2048]{0:T(1024)S(1)} %select_maximum_fusion.2, f32[1024,2048]{1,0:T(8,128)} %get-tuple-element.243, f32[1024]{0:T(1024)S(1)} %rsqrt_multiply_fusion.2, s32[2048]{0:T(1024)S(1)} %get-tuple-element.276, s32[1024]{0:T(1024)S(1)} %iota_add_fusion.4, ...), kind=kLoop, calls=%fused_computation.42.clone.1 | loop fusion | flops 16775168 | bytes 12616704 | tf_op jit(solution)/shard_map/cond/branch_0_fun/while/body/eval_jaxpr/reduce_sum | solution.py:206
  156.7 2.0 fusion.29
  162.4 4.5 %fusion.26 = (f32[2048]{0:T(1024)S(1)}, f32[1024,2048]{1,0:T(8,128)}) fusion(f32[1024]{0:T(1024)S(1)} %rsqrt_multiply_fusion.2, s32[2048]{0:T(1024)S(1)} %get-tuple-element.276, s32[1024]{0:T(1024)S(1)} %iota_add_fusion.4, pred[1024]{0:T(1024)(128)(4,1)S(1)} %broadcast_compare_fusion.3, bf16[2048,128]{1,0:T(8,128)(2,1)S(1)} %get-tuple-element.278, ...), kind=kOutput, calls=%fused_computation.4.clone.1 | convolution fusion | flops 547354624 | bytes 9200640 | tf_op jit(solution)/shard_map/cond/branch_0_fun/while/body/eval_jaxpr/dot_general | solution.py:198
  167.0 6.3 %fusion.27 = (f32[2048]{0:T(1024)S(1)}, bf16[2048,1024]{0,1:T(8,128)(2,1)S(1)}) fusion(f32[2048]{0:T(1024)S(1)} %select_maximum_fusion.2, f32[1024,2048]{1,0:T(8,128)} %get-tuple-element.243, f32[1024]{0:T(1024)S(1)} %rsqrt_multiply_fusion.2, s32[2048]{0:T(1024)S(1)} %get-tuple-element.276, s32[1024]{0:T(1024)S(1)} %iota_add_fusion.4, ...), kind=kLoop, calls=%fused_computation.42.clone.1 | loop fusion | flops 16775168 | bytes 12616704 | tf_op jit(solution)/shard_map/cond/branch_0_fun/while/body/eval_jaxpr/reduce_sum | solution.py:206
  173.3 2.0 fusion.29
  179.0 4.5 %fusion.26 = (f32[2048]{0:T(1024)S(1)}, f32[1024,2048]{1,0:T(8,128)}) fusion(f32[1024]{0:T(1024)S(1)} %rsqrt_multiply_fusion.2, s32[2048]{0:T(1024)S(1)} %get-tuple-element.276, s32[1024]{0:T(1024)S(1)} %iota_add_fusion.4, pred[1024]{0:T(1024)(128)(4,1)S(1)} %broadcast_compare_fusion.3, bf16[2048,128]{1,0:T(8,128)(2,1)S(1)} %get-tuple-element.278, ...), kind=kOutput, calls=%fused_computation.4.clone.1 | convolution fusion | flops 547354624 | bytes 9200640 | tf_op jit(solution)/shard_map/cond/branch_0_fun/while/body/eval_jaxpr/dot_general | solution.py:198
  183.6 6.3 %fusion.27 = (f32[2048]{0:T(1024)S(1)}, bf16[2048,1024]{0,1:T(8,128)(2,1)S(1)}) fusion(f32[2048]{0:T(1024)S(1)} %select_maximum_fusion.2, f32[1024,2048]{1,0:T(8,128)} %get-tuple-element.243, f32[1024]{0:T(1024)S(1)} %rsqrt_multiply_fusion.2, s32[2048]{0:T(1024)S(1)} %get-tuple-element.276, s32[1024]{0:T(1024)S(1)} %iota_add_fusion.4, ...), kind=kLoop, calls=%fused_computation.42.clone.1 | loop fusion | flops 16775168 | bytes 12616704 | tf_op jit(solution)/shard_map/cond/branch_0_fun/while/body/eval_jaxpr/reduce_sum | solution.py:206
  189.9 2.0 fusion.29
  195.6 4.5 %fusion.26 = (f32[2048]{0:T(1024)S(1)}, f32[1024,2048]{1,0:T(8,128)}) fusion(f32[1024]{0:T(1024)S(1)} %rsqrt_multiply_fusion.2, s32[2048]{0:T(1024)S(1)} %get-tuple-element.276, s32[1024]{0:T(1024)S(1)} %iota_add_fusion.4, pred[1024]{0:T(1024)(128)(4,1)S(1)} %broadcast_compare_fusion.3, bf16[2048,128]{1,0:T(8,128)(2,1)S(1)} %get-tuple-element.278, ...), kind=kOutput, calls=%fused_computation.4.clone.1 | convolution fusion | flops 547354624 | bytes 9200640 | tf_op jit(solution)/shard_map/cond/branch_0_fun/while/body/eval_jaxpr/dot_general | solution.py:198
  200.2 6.3 %fusion.27 = (f32[2048]{0:T(1024)S(1)}, bf16[2048,1024]{0,1:T(8,128)(2,1)S(1)}) fusion(f32[2048]{0:T(1024)S(1)} %select_maximum_fusion.2, f32[1024,2048]{1,0:T(8,128)} %get-tuple-element.243, f32[1024]{0:T(1024)S(1)} %rsqrt_multiply_fusion.2, s32[2048]{0:T(1024)S(1)} %get-tuple-element.276, s32[1024]{0:T(1024)S(1)} %iota_add_fusion.4, ...), kind=kLoop, calls=%fused_computation.42.clone.1 | loop fusion | flops 16775168 | bytes 12616704 | tf_op jit(solution)/shard_map/cond/branch_0_fun/while/body/eval_jaxpr/reduce_sum | solution.py:206
  206.5 2.0 fusion.29
  212.2 4.5 %fusion.26 = (f32[2048]{0:T(1024)S(1)}, f32[1024,2048]{1,0:T(8,128)}) fusion(f32[1024]{0:T(1024)S(1)} %rsqrt_multiply_fusion.2, s32[2048]{0:T(1024)S(1)} %get-tuple-element.276, s32[1024]{0:T(1024)S(1)} %iota_add_fusion.4, pred[1024]{0:T(1024)(128)(4,1)S(1)} %broadcast_compare_fusion.3, bf16[2048,128]{1,0:T(8,128)(2,1)S(1)} %get-tuple-element.278, ...), kind=kOutput, calls=%fused_computation.4.clone.1 | convolution fusion | flops 547354624 | bytes 9200640 | tf_op jit(solution)/shard_map/cond/branch_0_fun/while/body/eval_jaxpr/dot_general | solution.py:198
  216.8 6.3 %fusion.27 = (f32[2048]{0:T(1024)S(1)}, bf16[2048,1024]{0,1:T(8,128)(2,1)S(1)}) fusion(f32[2048]{0:T(1024)S(1)} %select_maximum_fusion.2, f32[1024,2048]{1,0:T(8,128)} %get-tuple-element.243, f32[1024]{0:T(1024)S(1)} %rsqrt_multiply_fusion.2, s32[2048]{0:T(1024)S(1)} %get-tuple-element.276, s32[1024]{0:T(1024)S(1)} %iota_add_fusion.4, ...), kind=kLoop, calls=%fused_computation.42.clone.1 | loop fusion | flops 16775168 | bytes 12616704 | tf_op jit(solution)/shard_map/cond/branch_0_fun/while/body/eval_jaxpr/reduce_sum | solution.py:206
  223.1 2.0 fusion.29
  227.5 5.7 %all-to-all-start = ((bf16[8,2,128,128]{3,2,1,0:T(8,128)(2,1)}), bf16[8,2,128,128]{3,2,1,0:T(8,128)(2,1)S(1)}, u32[]{:S(2)}, u32[]{:S(2)}) async-start(bf16[8,2,128,128]{3,2,1,0:T(8,128)(2,1)} %copy.7), calls=%async_computation | async-start | bytes 1048576 | tf_op jit(solution)/shard_map/all_to_all | solution.py:317
  233.9 10.4 %all-to-all-done.near_ref.far_ref = bf16[8,2,128,128]{3,2,1,0:T(8,128)(2,1)S(1)} async-done(((bf16[8,2,128,128]{3,2,1,0:T(8,128)(2,1)}), bf16[8,2,128,128]{3,2,1,0:T(8,128)(2,1)S(1)}, u32[]{:S(2)}, u32[]{:S(2)}) %all-to-all-start) | async-done | bytes 524320 | tf_op jit(solution)/shard_map/all_to_all | solution.py:317
  245.1 7.3 %output_given.1 = bf16[8,128,256]{2,1,0:T(8,128)(2,1)} custom-call(s32[2]{0:T(128)} %pad_add_fusion.2.scal_ref, bf16[8,2,128,128]{3,2,1,0:T(8,128)(2,1)} %copy-done.1, bf16[8,2,128,128]{3,2,1,0:T(8,128)(2,1)} %copy-done.1, bf16[512,2048]{1,0:T(8,128)(2,1)} %all-gather.3.cloned.1.call-done.w_near_ref, bf16[512,2048]{1,0:T(8,128)(2,1)} %all-gather.5.cloned.1.call-done.w_far_ref), custom_call_target="tpu_custom_call" | custom-call | flops 536870912 | bytes 5242880 | tf_op jit(solution)/shard_map/output_given/pallas_call | solution.py:236
  253.0 7.4 %output_own.1 = f32[8,128,256]{2,1,0:T(8,128)} custom-call(s32[2]{0:T(128)} %pad_add_fusion.1.scal_ref, bf16[8,2,128,128]{3,2,1,0:T(8,128)(2,1)} %copy-done.1, bf16[8,2,128,128]{3,2,1,0:T(8,128)(2,1)} %copy-done.1, bf16[512,2048]{1,0:T(8,128)(2,1)} %all-gather.3.cloned.1.call-done.w_near_ref, bf16[512,2048]{1,0:T(8,128)(2,1)} %all-gather.5.cloned.1.call-done.w_far_ref), custom_call_target="tpu_custom_call" | custom-call | flops 536870912 | bytes 5242880 | tf_op jit(solution)/shard_map/output_own/pallas_call | solution.py:236
  260.4 1.3 add_convert_fusion
  261.8 15.0 %all_to_all.10 = bf16[8,128,256]{2,1,0:T(8,128)(2,1)S(1)} all-to-all(bf16[8,128,256]{2,1,0:T(8,128)(2,1)S(1)} %add_convert_fusion), channel_id=1, replica_groups=mesh['seq'=8,'head'=8,'batch'=2] {'head'}, dimensions={0} | all-to-all | bytes 1048576 | tf_op jit(solution)/shard_map/all_to_all | solution.py:326
  (122 shorter events, 38.7 us)
Async XLA Ops:
  6.5 1.2 copy-start
  6.5 237.7 %all-gather.3.cloned.1.call-start = ((), (), s32[]{:S(2)}) async-start(), calls=%async_computation.2 | async-start | bytes 2621440 | tf_op jit(solution)/shard_map/all_gather | solution.py:279
  8.6 235.7 %all-gather.5.cloned.1.call-start = ((), (), s32[]{:S(2)}) async-start(), calls=%async_computation.3 | async-start | bytes 2621440 | tf_op jit(solution)/shard_map/all_gather | solution.py:280
  8.7 15.1 %collective-permute-start.7 = (bf16[128,2048]{1,0:T(8,128)(2,1)}, bf16[128,2048]{1,0:T(8,128)(2,1)S(1)}, u32[]{:S(2)}, u32[]{:S(2)}) collective-permute-start(bf16[128,2048]{1,0:T(8,128)(2,1)} %constant_dynamic-slice_fusion), channel_id=1, source_target_pairs={{0,9},{1,8},{2,11},{3,10},{4,13},{5,12},{6,15},{7,14},{8,1},{9,0},... | collective-permute-start | bytes 1572872 | tf_op jit(solution)/shard_map/ppermute | solution.py:274
  23.7 0.8 copy-start.3
  29.8 6.6 %collective-permute-start = (bf16[1024,256]{1,0:T(8,128)(2,1)}, bf16[1024,256]{1,0:T(8,128)(2,1)S(1)}, u32[]{:S(2)}, u32[]{:S(2)}) collective-permute-start(bf16[1024,256]{1,0:T(8,128)(2,1)} %project_given.1), channel_id=1, source_target_pairs={{0,16},{16,0},{32,48},{48,32},{64,80},{80,64},{96,112},{112,96},{1... | collective-permute-start | bytes 1572872 | tf_op jit(solution)/shard_map/ppermute | solution.py:267
  34.2 17.7 %collective-permute-start.1 = (bf16[1024,256]{1,0:T(8,128)(2,1)S(1)}, bf16[1024,256]{1,0:T(8,128)(2,1)S(1)}, u32[]{:S(2)}, u32[]{:S(2)}) collective-permute-start(bf16[1024,256]{1,0:T(8,128)(2,1)S(1)} %project_own.1.refs_0_.refs_2_), channel_id=1, source_target_pairs={{0,32},{16,48},{32,64},{48,80},{64,96},{80,112},{96,0},{112,16},{1... | collective-permute-start | bytes 1572872 | tf_op jit(solution)/shard_map/ppermute | solution.py:270
  36.4 15.6 %collective-permute-start.2 = (bf16[1024,256]{1,0:T(8,128)(2,1)S(1)}, bf16[1024,256]{1,0:T(8,128)(2,1)S(1)}, u32[]{:S(2)}, u32[]{:S(2)}) collective-permute-start(bf16[1024,256]{1,0:T(8,128)(2,1)S(1)} %collective-permute-done.refs_1_.refs_3_), channel_id=1, source_target_pairs={{0,96},{16,112},{32,0},{48,16},{64,32},{80,48},{96,64},{112,80},{1... | collective-permute-start | bytes 1572872 | tf_op jit(solution)/shard_map/ppermute | solution.py:270
  38.6 23.9 %collective-permute-start.4 = (bf16[1024,256]{1,0:T(8,128)(2,1)S(1)}, bf16[1024,256]{1,0:T(8,128)(2,1)}, u32[]{:S(2)}, u32[]{:S(2)}) collective-permute-start(bf16[1024,256]{1,0:T(8,128)(2,1)S(1)} %project_own.1.refs_0_.refs_2_), channel_id=1, source_target_pairs={{0,96},{16,112},{32,0},{48,16},{64,32},{80,48},{96,64},{112,80},{1... | collective-permute-start | bytes 1572872 | tf_op jit(solution)/shard_map/ppermute | solution.py:270
  40.5 22.1 %collective-permute-start.3 = (bf16[1024,256]{1,0:T(8,128)(2,1)S(1)}, bf16[1024,256]{1,0:T(8,128)(2,1)}, u32[]{:S(2)}, u32[]{:S(2)}) collective-permute-start(bf16[1024,256]{1,0:T(8,128)(2,1)S(1)} %collective-permute-done.refs_1_.refs_3_), channel_id=1, source_target_pairs={{0,32},{16,48},{32,64},{48,80},{64,96},{80,112},{96,0},{112,16},{1... | collective-permute-start | bytes 1572872 | tf_op jit(solution)/shard_map/ppermute | solution.py:270
  51.9 26.5 %collective-permute-start.5 = (bf16[1024,256]{1,0:T(8,128)(2,1)S(1)}, bf16[1024,256]{1,0:T(8,128)(2,1)S(1)}, u32[]{:S(2)}, u32[]{:S(2)}) collective-permute-start(bf16[1024,256]{1,0:T(8,128)(2,1)S(1)} %collective-permute-done.1.refs_2_), channel_id=1, source_target_pairs={{0,32},{16,48},{32,64},{48,80},{64,96},{80,112},{96,0},{112,16},{1... | collective-permute-start | bytes 1572872 | tf_op jit(solution)/shard_map/ppermute | solution.py:270
  52.0 26.4 %collective-permute-start.6 = (bf16[1024,256]{1,0:T(8,128)(2,1)S(1)}, bf16[1024,256]{1,0:T(8,128)(2,1)S(1)}, u32[]{:S(2)}, u32[]{:S(2)}) collective-permute-start(bf16[1024,256]{1,0:T(8,128)(2,1)S(1)} %collective-permute-done.2.refs_3_), channel_id=1, source_target_pairs={{0,96},{16,112},{32,0},{48,16},{64,32},{80,48},{96,64},{112,80},{1... | collective-permute-start | bytes 1572872 | tf_op jit(solution)/shard_map/ppermute | solution.py:270
  90.2 2.0 copy-start.2
  227.5 16.8 %all-to-all-start = ((bf16[8,2,128,128]{3,2,1,0:T(8,128)(2,1)}), bf16[8,2,128,128]{3,2,1,0:T(8,128)(2,1)S(1)}, u32[]{:S(2)}, u32[]{:S(2)}) async-start(bf16[8,2,128,128]{3,2,1,0:T(8,128)(2,1)} %copy.7), calls=%async_computation | async-start | bytes 1048576 | tf_op jit(solution)/shard_map/all_to_all | solution.py:317
  244.3 0.8 copy-start.1
  252.4 8.1 %collective-permute-start.8 = (bf16[8,128,256]{2,1,0:T(8,128)(2,1)}, bf16[8,128,256]{2,1,0:T(8,128)(2,1)S(1)}, u32[]{:S(2)}, u32[]{:S(2)}) collective-permute-start(bf16[8,128,256]{2,1,0:T(8,128)(2,1)} %output_given.1), channel_id=1, source_target_pairs={{0,16},{16,0},{32,48},{48,32},{64,80},{80,64},{96,112},{112,96},{1... | collective-permute-start | bytes 1572872 | tf_op jit(solution)/shard_map/ppermute | solution.py:267
Sparse Core Ops, SparseCore 0:
  9.0 33.3 all-gather.2
  44.0 30.8 all-gather.4

commit v2 on v0

v2 whole, which is shorter than its diff:
```python
import functools
import math

import jax
import jax.numpy as jnp
from jax import lax
from jax.experimental import pallas as pl
from jax.experimental.pallas import tpu as pltpu
from jax.sharding import PartitionSpec as P

HEAD_DIM = 128
LOG2E = 1.4426950408889634
NORM_LIMIT = 60.0
EXTRA = 16
NT = (((1,), (1,)), ((), ()))
VMEM = 56 * 2**20
HBM = pl.BlockSpec(memory_space=pl.ANY)
SMEM = pl.BlockSpec(memory_space=pltpu.SMEM)
F32 = jnp.float32
BF16 = jnp.bfloat16


def own_core():
    return lax.rem(lax.axis_index("seq"), 2)


def block_start(by, other, rows):
    seq = lax.axis_index("seq")
    place = lax.rem(lax.div(seq, 2) + by, 4) * 2
    core = lax.rem(seq, 2)
    return (place + (1 - core if other else core)) * rows


def start_all(copies):
    for copy in copies:
        copy.start()
    return copies


def project_kernel(x_ref, ws_ref, wv_ref, own_ref, given_ref, x_scr, ws_scr, wv_scr, out_scr, sem):
    rows, _ = x_ref.shape
    cuts = x_scr.shape[0]
    step = rows // cuts
    weights = start_all(
        [
            pltpu.make_async_copy(ws_ref, ws_scr, sem.at[0]),
            pltpu.make_async_copy(wv_ref, wv_scr, sem.at[1]),
        ]
    )
    tokens = start_all(
        [
            pltpu.make_async_copy(x_ref.at[pl.ds(i * step, step)], x_scr.at[i], sem.at[2 + i])
            for i in range(cuts)
        ]
    )
    wide = 2 * HEAD_DIM
    row = lax.broadcasted_iota(jnp.int32, (EXTRA, wide), 0)
    extra = [jnp.zeros((EXTRA, wide), F32) for _ in range(2)]
    largest = [jnp.zeros((8, wide), F32) for _ in range(2)]
    ones = jnp.ones((8, HEAD_DIM), BF16)
    for copy in weights:
        copy.wait()
    for i in range(cuts):
        tokens[i].wait()
        x = x_scr[i]
        shared = jnp.dot(x, ws_scr[...], preferred_element_type=F32).astype(BF16)
        values = jnp.dot(x, wv_scr[...], preferred_element_type=F32).astype(BF16)
        for h in range(2):
            cols = slice(h * HEAD_DIM, (h + 1) * HEAD_DIM)
            keys = shared[:, cols]
            out_scr[h, i * step : (i + 1) * step, :HEAD_DIM] = keys
            out_scr[h, i * step : (i + 1) * step, HEAD_DIM:] = values[:, cols]
            square = keys.astype(F32) * keys.astype(F32)
            high = square.astype(BF16)
            low = (square - high.astype(F32)).astype(BF16)
            total = lax.dot_general(ones, high, NT, preferred_element_type=F32)
            total += lax.dot_general(ones, low, NT, preferred_element_type=F32)
            for j in range(step // wide):
                part = total[:, j * wide : (j + 1) * wide]
                largest[h] = jnp.maximum(largest[h], part)
                factor = lax.rsqrt(part / HEAD_DIM + 1e-06) * (LOG2E / math.sqrt(HEAD_DIM))
                first = factor.astype(BF16).astype(F32)
                at = i * (step // wide) + j
                first16 = jnp.concatenate([first, first])
                second16 = jnp.concatenate([factor - first, factor - first])
                extra[h] = jnp.where(row == at, first16, extra[h])
                extra[h] = jnp.where(row == 4 + at, second16, extra[h])
    for h in range(2):
        top = jnp.broadcast_to(jnp.max(largest[h]), (EXTRA, wide))
        out_scr[h, rows:, :] = jnp.where(row >= 8, top, extra[h]).astype(BF16)
    core = own_core()
    for copy in start_all(
        [
            pltpu.make_async_copy(out_scr.at[core], own_ref, sem.at[0]),
            pltpu.make_async_copy(out_scr.at[1 - core], given_ref, sem.at[1]),
        ]
    ):
        copy.wait()


def project(tokens, w_shared, w_value):
    rows, width = tokens.shape
    cuts = 2
    out = jax.ShapeDtypeStruct((rows + EXTRA, 2 * HEAD_DIM), BF16)
    return pl.pallas_call(
        project_kernel,
        in_specs=[HBM] * 3,
        out_specs=(HBM, HBM),
        out_shape=(out, out),
        scratch_shapes=[
            pltpu.VMEM((cuts, rows // cuts, width), BF16),
            pltpu.VMEM(w_shared.shape, BF16),
            pltpu.VMEM(w_value.shape, BF16),
            pltpu.VMEM((2, rows + EXTRA, 2 * HEAD_DIM), BF16),
            pltpu.SemaphoreType.DMA((2 + cuts,)),
        ],
        compiler_params=pltpu.CompilerParams(vmem_limit_bytes=VMEM),
        cost_estimate=pl.CostEstimate(
            flops=2 * rows * width * 512, bytes_accessed=7 * 2**20, transcendentals=0
        ),
        name="project",
    )(tokens, w_shared, w_value)


def spread_kernel(w_ref, after_ref, out_ref, sem):
    del after_ref
    mine = w_ref.at[pl.ds(pl.multiple_of(own_core() * HEAD_DIM, HEAD_DIM), HEAD_DIM)]
    for copy in start_all(
        [pltpu.make_async_copy(mine, out_ref.at[i], sem.at[i]) for i in range(4)]
    ):
        copy.wait()


def spread(w_output, after):
    return pl.pallas_call(
        spread_kernel,
        in_specs=[HBM] * 2,
        out_specs=HBM,
        out_shape=jax.ShapeDtypeStruct((4, HEAD_DIM, w_output.shape[1]), BF16),
        scratch_shapes=[pltpu.SemaphoreType.DMA((4,))],
        name="spread",
    )(w_output, after)


def attend_kernel(places, first, last, doc_ref, *refs):
    count = len(places)
    if first:
        kv_refs, refs = refs[:count], refs[count:]
        out_ref, kv_scr, acc, sem, acc_sem = refs
        q_of = lambda q: kv_scr[q, :-EXTRA, :HEAD_DIM]
        copies = []
    else:
        q_refs, kv_refs, refs = refs[:2], refs[2 : 2 + count], refs[2 + count :]
        state_ref, refs = refs[0], refs[1:]
        if last:
            rest, refs = refs[:4], refs[4:]
            out_ref, kv_scr, acc, sem, acc_sem, q_scr, ctx_scr, peak, weight_sum = refs
        else:
            out_ref, kv_scr, acc, sem, acc_sem, q_scr = refs
        q_of = lambda q: q_scr[q, :-EXTRA, :]
        copies = start_all(
            [
                pltpu.make_async_copy(q_refs[q].at[:, pl.ds(0, HEAD_DIM)], q_scr.at[q], acc_sem.at[2 + q])
                for q in range(2)
            ]
        )
    rows = kv_scr.shape[1] - EXTRA
    tile = 512
    blocks = start_all(
        [pltpu.make_async_copy(kv_refs[i], kv_scr.at[i], sem.at[i]) for i in range(count)]
    )
    if not first:
        copies += start_all(
            [pltpu.make_async_copy(state_ref.at[q], acc.at[q], acc_sem.at[q]) for q in range(2)]
        )
    else:
        acc[...] = jnp.zeros_like(acc)
    for copy in copies:
        copy.wait()
    doc_len = doc_ref[0]
    q_starts = [block_start(0, other, rows) for other in (False, True)]
    active = jnp.minimum(q_starts[0], q_starts[1]) < doc_len
    if first:
        for copy in blocks:
            copy.wait()
    for i in range(count):
        if not first:
            blocks[i].wait()
        start = block_start(*places[i], rows)

        @pl.when(active & (start < doc_len))
        def _(i=i, start=start):
            extra = kv_scr[i, rows : rows + 8, :].astype(F32)
            factor = extra[0:4] + extra[4:8]
            for q in range(2):
                queries = q_of(q)
                total = acc[q]
                for cut in range(rows // tile):
                    keys = slice(cut * tile, (cut + 1) * tile)
                    each = tile // 256
                    scale = jnp.concatenate(
                        [factor[cut * each + j : cut * each + j + 1] for j in range(each)], axis=1
                    )
                    place = lax.broadcasted_iota(jnp.int32, (1, tile), 1) + (start + cut * tile)
                    bias = jnp.where(place < doc_len, 0.0, -1e30)
                    scores = lax.dot_general(
                        queries, kv_scr[i, keys, :HEAD_DIM], NT, preferred_element_type=F32
                    )
                    weights = jnp.exp2(scores * scale + bias)
                    if first and i == q:
                        weights = jnp.where(
                            lax.broadcasted_iota(jnp.int32, weights.shape, 0)
                            == lax.broadcasted_iota(jnp.int32, weights.shape, 1) + cut * tile,
                            0.0,
                            weights,
                        )
                    values = jnp.concatenate(
                        [kv_scr[i, keys, HEAD_DIM:], jnp.ones((tile, HEAD_DIM), BF16)], axis=1
                    )
                    total += jnp.dot(weights.astype(BF16), values, preferred_element_type=F32)
                acc[q] = total

    if not last:
        for copy in start_all(
            [pltpu.make_async_copy(acc.at[q], out_ref.at[q], acc_sem.at[q]) for q in range(2)]
        ):
            copy.wait()
        return

    norm = jnp.maximum(
        jnp.max(q_scr[0, rows + 8 :, :].astype(F32)), jnp.max(q_scr[1, rows + 8 :, :].astype(F32))
    )

    @pl.when(norm > NORM_LIMIT**2)
    def _():
        peak[...] = jnp.full_like(peak, -1e30)
        weight_sum[...] = jnp.zeros_like(weight_sum)
        acc[...] = jnp.zeros_like(acc)
        near = ((3, False), (3, True), (1, False), (1, True))
        everything = [
            (q_refs[0], (0, False)),
            (q_refs[1], (0, True)),
            *zip(rest, near),
            *zip(kv_refs, places),
        ]
        small = 256
        for block_ref, place in everything:
            pltpu.sync_copy(block_ref, kv_scr.at[0])
            key_start = block_start(*place, rows)
            extra = kv_scr[0, rows : rows + 8, :].astype(F32)
            factor = extra[0:4] + extra[4:8]

            def absorb(at, carry, key_start=key_start, factor=factor):
                q = lax.div(at, rows // small)
                low = pl.multiple_of(lax.rem(at, rows // small) * small, small)
                here = pl.ds(low, small)
                query_start = jnp.where(q == 0, q_starts[0], q_starts[1]) + low
                for cut in range(rows // small):
                    keys = slice(cut * small, (cut + 1) * small)
                    scores = lax.dot_general(
                        q_scr[q, here, :], kv_scr[0, keys, :HEAD_DIM], NT, preferred_element_type=F32
                    )
                    key_pos = lax.broadcasted_iota(jnp.int32, scores.shape, 1) + (
                        key_start + cut * small
                    )
                    query_pos = lax.broadcasted_iota(jnp.int32, scores.shape, 0) + query_start
                    allowed = (key_pos < doc_len) & (key_pos != query_pos)
                    scores = jnp.where(allowed, scores * factor[cut : cut + 1], -1e30)
                    old = peak[q, here, :]
                    new = jnp.maximum(old, jnp.max(scores, axis=1, keepdims=True))
                    weights = jnp.where(allowed, jnp.exp2(scores - new[:, :1]), 0.0)
                    rescale = jnp.exp2(old - new)
                    peak[q, here, :] = new
                    weight_sum[q, here, :] = weight_sum[q, here, :] * rescale + jnp.sum(
                        weights, axis=1, keepdims=True
                    )
                    acc[q, here, :HEAD_DIM] = acc[q, here, :HEAD_DIM] * rescale + jnp.dot(
                        weights.astype(BF16), kv_scr[0, keys, HEAD_DIM:], preferred_element_type=F32
                    )
                return carry

            lax.fori_loop(0, 2 * rows // small, absorb, 0)
        for q in range(2):
            acc[q, :, HEAD_DIM:] = weight_sum[q]

    core = own_core()
    outs = []
    for q in range(2):
        total = acc[q]
        inside = lax.broadcasted_iota(jnp.int32, (rows, HEAD_DIM), 0) + q_starts[q] < doc_len
        mixed = jnp.where(inside, total[:, :HEAD_DIM] / total[:, HEAD_DIM:], 0.0)
        ctx_scr[q] = mixed.astype(BF16).reshape(ctx_scr.shape[1:])
        block = core if q == 0 else 1 - core
        outs += start_all(
            [pltpu.make_async_copy(ctx_scr.at[q], out_ref.at[:, block], acc_sem.at[q])]
        )
    for copy in outs:
        copy.wait()


def attend(doc_length, queries, blocks, places, state, rest, name):
    rows = blocks[0].shape[0] - EXTRA
    count = len(blocks)
    first, last = state is None, rest is not None
    out_shape = jax.ShapeDtypeStruct((2, rows, 2 * HEAD_DIM), F32)
    scratch = [
        pltpu.VMEM((count, rows + EXTRA, 2 * HEAD_DIM), BF16),
        pltpu.VMEM(out_shape.shape, F32),
        pltpu.SemaphoreType.DMA((count,)),
        pltpu.SemaphoreType.DMA((4,)),
    ]
    args = list(blocks)
    if not first:
        args = [*queries, *blocks, state]
        scratch.append(pltpu.VMEM((2, rows + EXTRA, HEAD_DIM), BF16))
    if last:
        args += rest
        out_shape = jax.ShapeDtypeStruct((4, 2, rows // 4, HEAD_DIM), BF16)
        scratch += [
            pltpu.VMEM((2, 4, rows // 4, HEAD_DIM), BF16),
            pltpu.VMEM((2, rows, HEAD_DIM), F32),
            pltpu.VMEM((2, rows, HEAD_DIM), F32),
        ]
    return pl.pallas_call(
        functools.partial(attend_kernel, places, first, last),
        in_specs=[SMEM] + [HBM] * len(args),
        out_specs=HBM,
        out_shape=out_shape,
        scratch_shapes=scratch,
        compiler_params=pltpu.CompilerParams(vmem_limit_bytes=VMEM),
        cost_estimate=pl.CostEstimate(
            flops=16 * rows * rows * count * HEAD_DIM,
            bytes_accessed=4 * 2**20,
            transcendentals=0,
        ),
        name=name,
    )(doc_length, *args)


def output_kernel(ctx_ref, got_ref, w_ref, w_got_ref, out_ref, left_scr, w_scr, out_scr, sem, out_sem):
    core = own_core()
    width = w_ref.shape[2]
    cuts = out_sem.shape[0]
    step = width // cuts
    lefts = start_all(
        [
            pltpu.make_async_copy(ctx_ref.at[:, core], left_scr.at[0], sem.at[2 * cuts]),
            pltpu.make_async_copy(got_ref.at[:, core], left_scr.at[1], sem.at[2 * cuts + 1]),
        ]
    )
    weights = []
    for i in range(cuts):
        cols = pl.ds(i * step, step)
        weights.append(
            start_all(
                [
                    pltpu.make_async_copy(ref.at[:, :, cols], w_scr.at[at, :, :, cols], sem.at[2 * i + at])
                    for at, ref in enumerate((w_ref, w_got_ref))
                ]
            )
        )
    for copy in lefts:
        copy.wait()
    left = jnp.concatenate([left_scr[at, y] for at in range(2) for y in range(4)], axis=1)
    outs = []
    for i in range(cuts):
        for copy in weights[i]:
            copy.wait()
        cols = slice(i * step, (i + 1) * step)
        right = w_scr[:, :, :, cols].reshape(8 * HEAD_DIM, step)
        part = jnp.dot(left, right, preferred_element_type=F32).astype(BF16)
        for j in range(step // 256):
            out_scr[i * (step // 256) + j] = part[:, j * 256 : (j + 1) * 256]
        mine = pl.ds(i * (step // 256), step // 256)
        outs += start_all(
            [pltpu.make_async_copy(out_scr.at[mine], out_ref.at[mine], out_sem.at[i])]
        )
    for copy in outs:
        copy.wait()


def output(context, got, weights, weights_got):
    rows = context.shape[2]
    width = weights.shape[2]
    cuts = 4
    out_shape = jax.ShapeDtypeStruct((8, rows, width // 8), BF16)
    return pl.pallas_call(
        output_kernel,
        in_specs=[HBM] * 4,
        out_specs=HBM,
        out_shape=out_shape,
        scratch_shapes=[
            pltpu.VMEM((2, 4, rows, HEAD_DIM), BF16),
            pltpu.VMEM((2, *weights.shape), BF16),
            pltpu.VMEM(out_shape.shape, BF16),
            pltpu.SemaphoreType.DMA((2 * cuts + 2,)),
            pltpu.SemaphoreType.DMA((cuts,)),
        ],
        compiler_params=pltpu.CompilerParams(vmem_limit_bytes=VMEM),
        cost_estimate=pl.CostEstimate(
            flops=2 * rows * width * 1024, bytes_accessed=6 * 2**20, transcendentals=0
        ),
        name="output",
    )(context, got, weights, weights_got)


def body(tokens, w_shared, w_value, w_output, doc_length):
    def move(array, by, cross):
        return lax.ppermute(
            array, "seq", [(i, (i // 2 + by) % 4 * 2 + (i % 2 ^ cross)) for i in range(8)]
        )

    own, given = project(tokens, w_shared, w_value)
    peer = move(given, 0, 1)
    own_left, peer_right = move(own, 1, 0), move(given, -1, 1)
    peer_left, own_right = move(given, 1, 1), move(own, -1, 0)
    own_far, peer_far = move(own_left, 1, 0), move(peer_right, -1, 0)

    y_groups = [[0, 1, 2, 3], [4, 5, 6, 7]]
    weights = lax.all_to_all(
        spread(w_output, given), "head", 0, 0, axis_index_groups=y_groups, tiled=True
    )
    weights_got = move(weights, 0, 1)

    queries = (own, peer)
    near = (own_left, peer_left, own_right, peer_right)
    state = attend(doc_length, None, queries, ((0, False), (0, True)), None, None, "attend_here")
    state = attend(
        doc_length,
        queries,
        near,
        ((3, False), (3, True), (1, False), (1, True)),
        state,
        None,
        "attend_near",
    )
    context = attend(
        doc_length,
        queries,
        (own_far, peer_far),
        ((2, False), (2, True)),
        state,
        near,
        "attend_far",
    )
    context = lax.all_to_all(context, "head", 0, 0, axis_index_groups=y_groups, tiled=True)
    terms = output(context, move(context, 0, 1), weights, weights_got)
    terms = lax.all_to_all(terms, "head", 0, 0, tiled=True).astype(F32)
    result = (terms[:4] + terms[4:]).astype(BF16)
    return result.reshape(tokens.shape[0], result.shape[-1])


def solution(mesh):
    placed = (
        P(("batch", "seq"), None),
        P(None, "head"),
        P(None, "head"),
        P("head", None),
        P("batch"),
    )
    return jax.shard_map(
        body, mesh=mesh, in_specs=placed, out_specs=P(("batch", "seq"), "head"), check_vma=False
    )
```

time: 303 us -> 276 us (0.911); the launches traced: 302 us -> 271 us
  Pallas kernels: 0 us -> 203 us
  waiting for transfers between devices: 147 us -> 12.2 us
  matrix products: 71 us -> 0 us
  other arithmetic: 54 us -> 1.08 us
  blocking collectives: 0 us -> 36.7 us
  starting transfers between devices: 0.09 us -> 14.2 us
  local copies, waits for them, and re-layouts: 16.2 us -> 2.97 us
  between operations: 13.8 us -> 0.99 us
    pallas_call x0 -> x6, Pallas kernels: none -> 203 us  [the longest x3 128 us: attend(): pl.pallas_call(functools.partial(attend_kernel, places, first, last), in_...]
    reduce_scatter x1 -> x0, waiting for transfers between devices: 83.3 us -> none  [body(): lax.psum_scatter(projected.astype(jnp.bfloat16), 'head', scatter_dimensio...]
    dot_general x5 -> x0, matrix products: 71 us -> none  [the longest x1 30 us: absorb(): jnp.einsum('hqk,khd->qhd', unnorm.astype(jnp.bfloat16), key_values.reshap...]
    all_gather x2 -> x0, waiting for transfers between devices: 63.5 us -> none  [the longest x1 33.9 us: body(): remote_values = lax.all_gather(values, 'seq', axis=0, tiled=True)]
    reduce_sum x2 -> x0, other arithmetic: 39.1 us -> none  [the longest x1 24.2 us: absorb(): weight_sum = jnp.sum(unnorm, axis=-1)]
    all_to_all x0 -> x2, blocking collectives: none -> 36.7 us  [the longest x1 22.4 us: body(): terms = lax.all_to_all(terms, 'head', 0, 0, tiled=True).astype(F32)]
    ppermute x0 -> x9, waiting for transfers between devices: none -> 12.2 us  [move(): lax.ppermute(array, 'seq', [(i, (i // 2 + by) % 4 * 2 + (i % 2 ^ cross))...]
    and x1 -> x0, other arithmetic: 11.5 us -> none  [absorb(): (key_pos[None, :] < doc_len) & (key_pos[None, :] != query_pos[:, None])]
  transfers between devices with their start and end apart: 3 -> 10, of which waited for: 3 -> 2; matrix products, arithmetic and copies ran while one was open for 2% -> 0% of each run, Pallas kernels for 0% -> 47%
where the time goes in v2:
time: 276 us; the launch traced here: 271 us
  Pallas kernels  203 us (74%)
  blocking collectives  36.7 us (13%)
  starting transfers between devices  14.2 us (5%)
  waiting for transfers between devices  12.2 us (4%)
  local copies, waits for them, and re-layouts  2.97 us (1%)
    pallas_call x3, Pallas kernels, attend(): pl.pallas_call(functools.partial(attend_kernel, places, first, last), in_...  128 us
    pallas_call x1, Pallas kernels, spread(): pl.pallas_call(spread_kernel, in_specs=[HBM] * 2, out_specs=HBM, out_shap...  64.7 us
    all_to_all x1, blocking collectives, body(): terms = lax.all_to_all(terms, 'head', 0, 0, tiled=True).astype(F32)  22.4 us
    all_to_all x1, blocking collectives, body(): lax.all_to_all(context, 'head', 0, 0, axis_index_groups=y_groups, tiled=T...  14.3 us
    ppermute x9, waiting for transfers between devices, move(): lax.ppermute(array, 'seq', [(i, (i // 2 + by) % 4 * 2 + (i % 2 ^ cross))...  12.2 us
    ppermute x9, starting transfers between devices, move(): lax.ppermute(array, 'seq', [(i, (i // 2 + by) % 4 * 2 + (i % 2 ^ cross))...  9.51 us
    pallas_call x1, Pallas kernels, project(): pl.pallas_call(project_kernel, in_specs=[HBM] * 3, out_specs=(HBM, HBM),...  6.32 us
  transfers between devices with their start and end apart: 10, of which 2 were waited for; matrix products, arithmetic and copies ran while one was open for 0% of the time, Pallas kernels for 47%

profile of v2, /device:TPU:0, one launch (start us, length us, event | category | flops | bytes accessed | tf_op | source)
XLA Modules:
  0.0 271.2 jit_solution(14492946628073355397)
XLA Ops:
  0.0 6.3 %project.1 = (bf16[1040,256]{1,0:T(8,128)(2,1)}, bf16[1040,256]{1,0:T(8,128)(2,1)}) custom-call(bf16[1024,2048]{1,0:T(8,128)(2,1)} %x_ref.1, bf16[2048,256]{1,0:T(8,128)(2,1)} %ws_ref.1, bf16[2048,256]{1,0:T(8,128)(2,1)} %wv_ref.1), custom_call_target="tpu_custom_call" | custom-call | flops 2147483648 | bytes 7340032 | tf_op jit(solution)/shard_map/project/pallas_call | solution.py:105
  6.3 64.7 %spread.1 = bf16[4,128,2048]{2,1,0:T(8,128)(2,1)} custom-call(bf16[256,2048]{1,0:T(8,128)(2,1)} %w_ref.1, bf16[1040,256]{1,0:T(8,128)(2,1)} %get-tuple-element.8.after_ref), custom_call_target="tpu_custom_call" | custom-call | tf_op jit(solution)/shard_map/spread/pallas_call | solution.py:135
  71.0 0.0 copy-start.5
  71.0 0.0 copy-start.3
  71.0 4.7 %all-to-all-start.1 = ((bf16[4,128,2048]{2,1,0:T(8,128)(2,1)}), bf16[4,128,2048]{2,1,0:T(8,128)(2,1)S(1)}, u32[]{:S(2)}, u32[]{:S(2)}) async-start(bf16[4,128,2048]{2,1,0:T(8,128)(2,1)} %spread.1), calls=%async_computation.1 | async-start | bytes 4194304 | tf_op jit(solution)/shard_map/all_to_all | solution.py:420
  75.7 0.0 copy-done.5
  75.7 1.9 collective-permute-start.1
  77.6 0.0 copy-done.3
  77.6 1.4 collective-permute-start.3
  79.0 1.0 collective-permute-start
  80.0 1.9 collective-permute-start.6
  81.9 0.0 collective-permute-start.5
  82.6 10.3 %collective-permute-done.1.refs_2_.refs_5_ = bf16[1040,256]{1,0:T(8,128)(2,1)} collective-permute-done((bf16[1040,256]{1,0:T(8,128)(2,1)S(1)}, bf16[1040,256]{1,0:T(8,128)(2,1)}, u32[]{:S(2)}, u32[]{:S(2)}) %collective-permute-start.1) | collective-permute-done | bytes 532512 | tf_op jit(solution)/shard_map/ppermute | solution.py:409
  92.8 0.0 collective-permute-start.2
  92.8 0.0 collective-permute-done.3.refs_5_.refs_8_
  92.8 3.2 %collective-permute-start.4 = (bf16[1040,256]{1,0:T(8,128)(2,1)}, bf16[1040,256]{1,0:T(8,128)(2,1)}, u32[]{:S(2)}, u32[]{:S(2)}) collective-permute-start(bf16[1040,256]{1,0:T(8,128)(2,1)} %collective-permute-done.3.refs_5_.refs_8_), channel_id=1, source_target_pairs={{0,96},{16,112},{32,0},{48,16},{64,32},{80,48},{96,64},{112,80},{1... | collective-permute-start | bytes 1597448 | tf_op jit(solution)/shard_map/ppermute | solution.py:409
  96.1 0.0 collective-permute-done.refs_1_
  96.1 0.0 copy-start.6
  96.1 0.8 copy-done.6
  96.9 7.5 %attend_here.1.refs_6_ = f32[2,1024,256]{2,1,0:T(8,128)} custom-call(s32[1]{0:T(128)S(6)} %copy.6.doc_ref, bf16[1040,256]{1,0:T(8,128)(2,1)} %get-tuple-element.7.refs_0_, bf16[1040,256]{1,0:T(8,128)(2,1)} %copy-done.6), custom_call_target="tpu_custom_call" | custom-call | flops 4294967296 | bytes 4194304 | tf_op jit(solution)/shard_map/attend_here/pallas_call | solution.py:324
  104.4 0.0 all-to-all-done.1.w_ref
  104.4 0.0 copy-start
  104.5 0.1 collective-permute-start.8
  104.6 0.0 collective-permute-done.6.refs_4_.refs_7_
  104.6 0.0 collective-permute-done.5.refs_3_.refs_6_
  104.6 12.0 %attend_near.1.refs_4_ = f32[2,1024,256]{2,1,0:T(8,128)} custom-call(s32[1]{0:T(128)S(6)} %copy.6.doc_ref, bf16[1040,256]{1,0:T(8,128)(2,1)} %get-tuple-element.7.refs_0_, bf16[1040,256]{1,0:T(8,128)(2,1)} %copy-done.6, bf16[1040,256]{1,0:T(8,128)(2,1)} %collective-permute-done.1.refs_2_.refs_5_, bf16[1040,256]{1,0:T(8,128)(2,1)} %collective-permute-done.5.refs_3_.refs_6_, ...), custom_call_target="tpu_custom_call" | custom-call | flops 8589934592 | bytes 4194304 | tf_op jit(solution)/shard_map/attend_near/pallas_call | solution.py:324
  116.6 0.0 copy-done
  116.6 0.0 collective-permute-done.2.refs_2_
  116.6 0.0 collective-permute-done.4.refs_3_
  116.6 108.6 %attend_far.1 = bf16[4,2,256,128]{3,2,1,0:T(8,128)(2,1)} custom-call(s32[1]{0:T(128)S(6)} %copy.6.doc_ref, bf16[1040,256]{1,0:T(8,128)(2,1)} %get-tuple-element.7.refs_0_, bf16[1040,256]{1,0:T(8,128)(2,1)} %copy-done.6, bf16[1040,256]{1,0:T(8,128)(2,1)} %collective-permute-done.2.refs_2_, bf16[1040,256]{1,0:T(8,128)(2,1)} %collective-permute-done.4.refs_3_, ...), custom_call_target="tpu_custom_call" | custom-call | flops 4294967296 | bytes 4194304 | tf_op jit(solution)/shard_map/attend_far/pallas_call | solution.py:324
  225.2 14.3 %all_to_all.15.ctx_ref = bf16[4,2,256,128]{3,2,1,0:T(8,128)(2,1)S(1)} all-to-all(bf16[4,2,256,128]{3,2,1,0:T(8,128)(2,1)} %attend_far.1), channel_id=1, replica_groups={{0,2,4,6},{8,10,12,14},{1,3,5,7},{9,11,13,15},{16,18,20,22},{24,26,28,3..., dimensions={0} | all-to-all | bytes 1048576 | tf_op jit(solution)/shard_map/all_to_all | solution.py:446
  239.5 0.0 copy-start.2
  239.5 0.0 collective-permute-start.7
  239.5 1.9 collective-permute-done.7.got_ref
  241.5 0.0 copy-start.4
  241.5 0.0 collective-permute-done.8.w_got_ref
  241.5 0.0 copy-done.2
  241.5 0.8 copy-done.4
  242.3 0.0 copy-start.1
  242.3 1.3 copy-done.1
  243.6 4.0 %output.1 = bf16[8,256,256]{2,1,0:T(8,128)(2,1)} custom-call(bf16[4,2,256,128]{3,2,1,0:T(8,128)(2,1)} %copy-done.2, bf16[4,2,256,128]{3,2,1,0:T(8,128)(2,1)} %copy-done.4, bf16[4,128,2048]{2,1,0:T(8,128)(2,1)} %copy-done, bf16[4,128,2048]{2,1,0:T(8,128)(2,1)} %copy-done.1), custom_call_target="tpu_custom_call" | custom-call | flops 1073741824 | bytes 6291456 | tf_op jit(solution)/shard_map/output/pallas_call | solution.py:387
  247.6 22.4 %all_to_all.16 = bf16[8,256,256]{2,1,0:T(8,128)(2,1)S(1)} all-to-all(bf16[8,256,256]{2,1,0:T(8,128)(2,1)} %output.1), channel_id=1, replica_groups=mesh['seq'=8,'head'=8,'batch'=2] {'head'}, dimensions={0} | all-to-all | bytes 2097152 | tf_op jit(solution)/shard_map/all_to_all | solution.py:448
  269.9 0.2 convert_element_type.6
  270.1 0.9 fusion
Async XLA Ops:
  71.0 4.7 %copy-start.5 = (bf16[1040,256]{1,0:T(8,128)(2,1)S(1)}, bf16[1040,256]{1,0:T(8,128)(2,1)}, u32[]{:S(2)}) copy-start(bf16[1040,256]{1,0:T(8,128)(2,1)} %get-tuple-element.7.refs_0_) | copy-start | bytes 1597444
  71.0 6.6 %copy-start.3 = (bf16[1040,256]{1,0:T(8,128)(2,1)S(1)}, bf16[1040,256]{1,0:T(8,128)(2,1)}, u32[]{:S(2)}) copy-start(bf16[1040,256]{1,0:T(8,128)(2,1)} %get-tuple-element.8.after_ref) | copy-start | bytes 1597444
  71.0 33.4 %all-to-all-start.1 = ((bf16[4,128,2048]{2,1,0:T(8,128)(2,1)}), bf16[4,128,2048]{2,1,0:T(8,128)(2,1)S(1)}, u32[]{:S(2)}, u32[]{:S(2)}) async-start(bf16[4,128,2048]{2,1,0:T(8,128)(2,1)} %spread.1), calls=%async_computation.1 | async-start | bytes 4194304 | tf_op jit(solution)/shard_map/all_to_all | solution.py:420
  75.7 17.1 %collective-permute-start.1 = (bf16[1040,256]{1,0:T(8,128)(2,1)S(1)}, bf16[1040,256]{1,0:T(8,128)(2,1)}, u32[]{:S(2)}, u32[]{:S(2)}) collective-permute-start(bf16[1040,256]{1,0:T(8,128)(2,1)S(1)} %copy-done.5), channel_id=1, source_target_pairs={{0,32},{16,48},{32,64},{48,80},{64,96},{80,112},{96,0},{112,16},{1... | collective-permute-start | bytes 1597448 | tf_op jit(solution)/shard_map/ppermute | solution.py:409
  77.6 15.2 %collective-permute-start.3 = (bf16[1040,256]{1,0:T(8,128)(2,1)S(1)}, bf16[1040,256]{1,0:T(8,128)(2,1)}, u32[]{:S(2)}, u32[]{:S(2)}) collective-permute-start(bf16[1040,256]{1,0:T(8,128)(2,1)S(1)} %copy-done.3), channel_id=1, source_target_pairs={{0,112},{16,96},{32,16},{48,0},{64,48},{80,32},{96,80},{112,64},{1... | collective-permute-start | bytes 1597448 | tf_op jit(solution)/shard_map/ppermute | solution.py:409
  79.0 17.1 %collective-permute-start = (bf16[1040,256]{1,0:T(8,128)(2,1)S(1)}, bf16[1040,256]{1,0:T(8,128)(2,1)S(1)}, u32[]{:S(2)}, u32[]{:S(2)}) collective-permute-start(bf16[1040,256]{1,0:T(8,128)(2,1)S(1)} %copy-done.3), channel_id=1, source_target_pairs={{0,16},{16,0},{32,48},{48,32},{64,80},{80,64},{96,112},{112,96},{1... | collective-permute-start | bytes 1597448 | tf_op jit(solution)/shard_map/ppermute | solution.py:409
  80.0 24.6 %collective-permute-start.6 = (bf16[1040,256]{1,0:T(8,128)(2,1)S(1)}, bf16[1040,256]{1,0:T(8,128)(2,1)}, u32[]{:S(2)}, u32[]{:S(2)}) collective-permute-start(bf16[1040,256]{1,0:T(8,128)(2,1)S(1)} %copy-done.5), channel_id=1, source_target_pairs={{0,96},{16,112},{32,0},{48,16},{64,32},{80,48},{96,64},{112,80},{1... | collective-permute-start | bytes 1597448 | tf_op jit(solution)/shard_map/ppermute | solution.py:409
  81.9 22.7 %collective-permute-start.5 = (bf16[1040,256]{1,0:T(8,128)(2,1)S(1)}, bf16[1040,256]{1,0:T(8,128)(2,1)}, u32[]{:S(2)}, u32[]{:S(2)}) collective-permute-start(bf16[1040,256]{1,0:T(8,128)(2,1)S(1)} %copy-done.3), channel_id=1, source_target_pairs={{0,48},{16,32},{32,80},{48,64},{64,112},{80,96},{96,16},{112,0},{1... | collective-permute-start | bytes 1597448 | tf_op jit(solution)/shard_map/ppermute | solution.py:409
  92.8 23.8 %collective-permute-start.2 = (bf16[1040,256]{1,0:T(8,128)(2,1)}, bf16[1040,256]{1,0:T(8,128)(2,1)}, u32[]{:S(2)}, u32[]{:S(2)}) collective-permute-start(bf16[1040,256]{1,0:T(8,128)(2,1)} %collective-permute-done.1.refs_2_.refs_5_), channel_id=1, source_target_pairs={{0,32},{16,48},{32,64},{48,80},{64,96},{80,112},{96,0},{112,16},{1... | collective-permute-start | bytes 1597448 | tf_op jit(solution)/shard_map/ppermute | solution.py:409
  92.8 23.8 %collective-permute-start.4 = (bf16[1040,256]{1,0:T(8,128)(2,1)}, bf16[1040,256]{1,0:T(8,128)(2,1)}, u32[]{:S(2)}, u32[]{:S(2)}) collective-permute-start(bf16[1040,256]{1,0:T(8,128)(2,1)} %collective-permute-done.3.refs_5_.refs_8_), channel_id=1, source_target_pairs={{0,96},{16,112},{32,0},{48,16},{64,32},{80,48},{96,64},{112,80},{1... | collective-permute-start | bytes 1597448 | tf_op jit(solution)/shard_map/ppermute | solution.py:409
  96.1 0.8 copy-start.6
  104.4 12.1 %copy-start = (bf16[4,128,2048]{2,1,0:T(8,128)(2,1)}, bf16[4,128,2048]{2,1,0:T(8,128)(2,1)S(1)}, u32[]{:S(2)}) copy-start(bf16[4,128,2048]{2,1,0:T(8,128)(2,1)S(1)} %all-to-all-done.1.w_ref) | copy-start | bytes 6291460
  104.5 137.0 %collective-permute-start.8 = (bf16[4,128,2048]{2,1,0:T(8,128)(2,1)S(1)}, bf16[4,128,2048]{2,1,0:T(8,128)(2,1)S(1)}, u32[]{:S(2)}, u32[]{:S(2)}) collective-permute-start(bf16[4,128,2048]{2,1,0:T(8,128)(2,1)S(1)} %all-to-all-done.1.w_ref), channel_id=1, source_target_pairs={{0,16},{16,0},{32,48},{48,32},{64,80},{80,64},{96,112},{112,96},{1... | collective-permute-start | bytes 6291464 | tf_op jit(solution)/shard_map/ppermute | solution.py:409
  239.5 1.9 copy-start.2
  239.5 1.9 collective-permute-start.7
  241.5 0.8 copy-start.4
  242.3 1.3 copy-start.1

commit v3 on v2

--- a/solution.py
+++ b/solution.py
@@ -14,7 +14,7 @@
 EXTRA = 16
 NT = (((1,), (1,)), ((), ()))
 VMEM = 56 * 2**20
-HBM = pl.BlockSpec(memory_space=pl.ANY)
+HBM = pl.BlockSpec(memory_space=pltpu.HBM)
 SMEM = pl.BlockSpec(memory_space=pltpu.SMEM)
 F32 = jnp.float32
 BF16 = jnp.bfloat16
@@ -37,7 +37,7 @@
     return copies
 
 
-def project_kernel(x_ref, ws_ref, wv_ref, own_ref, given_ref, x_scr, ws_scr, wv_scr, out_scr, sem):
+def project_kernel(x_ref, ws_ref, wv_ref, own_ref, given_ref, x_scr, ws_scr, wv_scr, out_scr, sem, out_sem):
     rows, _ = x_ref.shape
     cuts = x_scr.shape[0]
     step = rows // cuts
@@ -58,6 +58,18 @@
     extra = [jnp.zeros((EXTRA, wide), F32) for _ in range(2)]
     largest = [jnp.zeros((8, wide), F32) for _ in range(2)]
     ones = jnp.ones((8, HEAD_DIM), BF16)
+    core = own_core()
+    outs = []
+
+    def send(low, size):
+        here = pl.ds(low, size)
+        for h, ref in ((core, own_ref), (1 - core, given_ref)):
+            copy = pltpu.make_async_copy(
+                out_scr.at[h, here], ref.at[here], out_sem.at[len(outs)]
+            )
+            copy.start()
+            outs.append(copy)
+
     for copy in weights:
         copy.wait()
     for i in range(cuts):
@@ -67,40 +79,32 @@
         values = jnp.dot(x, wv_scr[...], preferred_element_type=F32).astype(BF16)
         for h in range(2):
             cols = slice(h * HEAD_DIM, (h + 1) * HEAD_DIM)
-            keys = shared[:, cols]
-            out_scr[h, i * step : (i + 1) * step, :HEAD_DIM] = keys
+            out_scr[h, i * step : (i + 1) * step, :HEAD_DIM] = shared[:, cols]
             out_scr[h, i * step : (i + 1) * step, HEAD_DIM:] = values[:, cols]
-            square = keys.astype(F32) * keys.astype(F32)
+        send(i * step, step)
+        for h in range(2):
+            keys = shared[:, h * HEAD_DIM : (h + 1) * HEAD_DIM].astype(F32)
+            square = keys * keys
             high = square.astype(BF16)
             low = (square - high.astype(F32)).astype(BF16)
             total = lax.dot_general(ones, high, NT, preferred_element_type=F32)
             total += lax.dot_general(ones, low, NT, preferred_element_type=F32)
-            for j in range(step // wide):
-                part = total[:, j * wide : (j + 1) * wide]
-                largest[h] = jnp.maximum(largest[h], part)
-                factor = lax.rsqrt(part / HEAD_DIM + 1e-06) * (LOG2E / math.sqrt(HEAD_DIM))
-                first = factor.astype(BF16).astype(F32)
-                at = i * (step // wide) + j
-                first16 = jnp.concatenate([first, first])
-                second16 = jnp.concatenate([factor - first, factor - first])
-                extra[h] = jnp.where(row == at, first16, extra[h])
-                extra[h] = jnp.where(row == 4 + at, second16, extra[h])
+            largest[h] = jnp.maximum(largest[h], total)
+            factor = lax.rsqrt(total / HEAD_DIM + 1e-06) * (LOG2E / math.sqrt(HEAD_DIM))
+            first = factor.astype(BF16).astype(F32)
+            extra[h] = jnp.where(row == i, jnp.concatenate([first] * 2), extra[h])
+            extra[h] = jnp.where(row == 4 + i, jnp.concatenate([factor - first] * 2), extra[h])
     for h in range(2):
         top = jnp.broadcast_to(jnp.max(largest[h]), (EXTRA, wide))
         out_scr[h, rows:, :] = jnp.where(row >= 8, top, extra[h]).astype(BF16)
-    core = own_core()
-    for copy in start_all(
-        [
-            pltpu.make_async_copy(out_scr.at[core], own_ref, sem.at[0]),
-            pltpu.make_async_copy(out_scr.at[1 - core], given_ref, sem.at[1]),
-        ]
-    ):
+    send(rows, EXTRA)
+    for copy in outs:
         copy.wait()
 
 
 def project(tokens, w_shared, w_value):
     rows, width = tokens.shape
-    cuts = 2
+    cuts = 4
     out = jax.ShapeDtypeStruct((rows + EXTRA, 2 * HEAD_DIM), BF16)
     return pl.pallas_call(
         project_kernel,
@@ -113,6 +117,7 @@
             pltpu.VMEM(w_value.shape, BF16),
             pltpu.VMEM((2, rows + EXTRA, 2 * HEAD_DIM), BF16),
             pltpu.SemaphoreType.DMA((2 + cuts,)),
+            pltpu.SemaphoreType.DMA((2 * cuts + 2,)),
         ],
         compiler_params=pltpu.CompilerParams(vmem_limit_bytes=VMEM),
         cost_estimate=pl.CostEstimate(
@@ -122,22 +127,24 @@
     )(tokens, w_shared, w_value)
 
 
-def spread_kernel(w_ref, after_ref, out_ref, sem):
+def spread_kernel(w_ref, after_ref, out_ref, scr, sem):
     del after_ref
     mine = w_ref.at[pl.ds(pl.multiple_of(own_core() * HEAD_DIM, HEAD_DIM), HEAD_DIM)]
+    pltpu.sync_copy(mine, scr)
     for copy in start_all(
-        [pltpu.make_async_copy(mine, out_ref.at[i], sem.at[i]) for i in range(4)]
+        [pltpu.make_async_copy(scr, out_ref.at[i], sem.at[i]) for i in range(4)]
     ):
         copy.wait()
 
 
 def spread(w_output, after):
+    piece = (HEAD_DIM, w_output.shape[1])
     return pl.pallas_call(
         spread_kernel,
         in_specs=[HBM] * 2,
         out_specs=HBM,
-        out_shape=jax.ShapeDtypeStruct((4, HEAD_DIM, w_output.shape[1]), BF16),
-        scratch_shapes=[pltpu.SemaphoreType.DMA((4,))],
+        out_shape=jax.ShapeDtypeStruct((4, *piece), BF16),
+        scratch_shapes=[pltpu.VMEM(piece, BF16), pltpu.SemaphoreType.DMA((4,))],
         name="spread",
     )(w_output, after)
 
@@ -151,10 +158,9 @@
         copies = []
     else:
         q_refs, kv_refs, refs = refs[:2], refs[2 : 2 + count], refs[2 + count :]
-        state_ref, refs = refs[0], refs[1:]
         if last:
-            rest, refs = refs[:4], refs[4:]
-            out_ref, kv_scr, acc, sem, acc_sem, q_scr, ctx_scr, peak, weight_sum = refs
+            states, rest, refs = refs[:2], refs[2:6], refs[6:]
+            out_ref, kv_scr, acc, sem, acc_sem, q_scr, sums, sums_sem, ctx_scr, peak, weight_sum = refs
         else:
             out_ref, kv_scr, acc, sem, acc_sem, q_scr = refs
         q_of = lambda q: q_scr[q, :-EXTRA, :]
@@ -169,12 +175,11 @@
     blocks = start_all(
         [pltpu.make_async_copy(kv_refs[i], kv_scr.at[i], sem.at[i]) for i in range(count)]
     )
-    if not first:
-        copies += start_all(
-            [pltpu.make_async_copy(state_ref.at[q], acc.at[q], acc_sem.at[q]) for q in range(2)]
-        )
-    else:
-        acc[...] = jnp.zeros_like(acc)
+    if last:
+        added = start_all(
+            [pltpu.make_async_copy(states[i], sums.at[i], sums_sem.at[i]) for i in range(2)]
+        )
+    acc[...] = jnp.zeros_like(acc)
     for copy in copies:
         copy.wait()
     doc_len = doc_ref[0]
@@ -227,6 +232,8 @@
             copy.wait()
         return
 
+    for copy in added:
+        copy.wait()
     norm = jnp.maximum(
         jnp.max(q_scr[0, rows + 8 :, :].astype(F32)), jnp.max(q_scr[1, rows + 8 :, :].astype(F32))
     )
@@ -236,6 +243,7 @@
         peak[...] = jnp.full_like(peak, -1e30)
         weight_sum[...] = jnp.zeros_like(weight_sum)
         acc[...] = jnp.zeros_like(acc)
+        sums[...] = jnp.zeros_like(sums)
         near = ((3, False), (3, True), (1, False), (1, True))
         everything = [
             (q_refs[0], (0, False)),
@@ -286,7 +294,7 @@
     core = own_core()
     outs = []
     for q in range(2):
-        total = acc[q]
+        total = acc[q] + (sums[0, q] + sums[1, q])
         inside = lax.broadcasted_iota(jnp.int32, (rows, HEAD_DIM), 0) + q_starts[q] < doc_len
         mixed = jnp.where(inside, total[:, :HEAD_DIM] / total[:, HEAD_DIM:], 0.0)
         ctx_scr[q] = mixed.astype(BF16).reshape(ctx_scr.shape[1:])
@@ -298,10 +306,10 @@
         copy.wait()
 
 
-def attend(doc_length, queries, blocks, places, state, rest, name):
+def attend(doc_length, queries, blocks, places, states, rest, name):
     rows = blocks[0].shape[0] - EXTRA
     count = len(blocks)
-    first, last = state is None, rest is not None
+    first, last = queries is None, rest is not None
     out_shape = jax.ShapeDtypeStruct((2, rows, 2 * HEAD_DIM), F32)
     scratch = [
         pltpu.VMEM((count, rows + EXTRA, 2 * HEAD_DIM), BF16),
@@ -311,10 +319,14 @@
     ]
     args = list(blocks)
     if not first:
-        args = [*queries, *blocks, state]
+        args = [*queries, *blocks]
         scratch.append(pltpu.VMEM((2, rows + EXTRA, HEAD_DIM), BF16))
     if last:
-        args += rest
+        args += [*states, *rest]
+        scratch += [
+            pltpu.VMEM((2, *out_shape.shape), F32),
+            pltpu.SemaphoreType.DMA((2,)),
+        ]
         out_shape = jax.ShapeDtypeStruct((4, 2, rows // 4, HEAD_DIM), BF16)
         scratch += [
             pltpu.VMEM((2, 4, rows // 4, HEAD_DIM), BF16),
@@ -414,33 +426,35 @@
     peer = move(given, 0, 1)
     own_left, peer_right = move(own, 1, 0), move(given, -1, 1)
     peer_left, own_right = move(given, 1, 1), move(own, -1, 0)
-    own_far, peer_far = move(own_left, 1, 0), move(peer_right, -1, 0)
 
     y_groups = [[0, 1, 2, 3], [4, 5, 6, 7]]
     weights = lax.all_to_all(
-        spread(w_output, given), "head", 0, 0, axis_index_groups=y_groups, tiled=True
-    )
-    weights_got = move(weights, 0, 1)
+        spread(w_output, peer), "head", 0, 0, axis_index_groups=y_groups, tiled=True
+    )
 
     queries = (own, peer)
-    near = (own_left, peer_left, own_right, peer_right)
-    state = attend(doc_length, None, queries, ((0, False), (0, True)), None, None, "attend_here")
-    state = attend(
+    here = attend(doc_length, None, queries, ((0, False), (0, True)), None, None, "attend_here")
+    own_left, peer_right, here = lax.optimization_barrier((own_left, peer_right, here))
+    own_far, peer_far = move(own_left, 1, 0), move(peer_right, -1, 0)
+    blocks = (own_left, peer_left, own_right, peer_right)
+    near = attend(
         doc_length,
         queries,
-        near,
+        blocks,
         ((3, False), (3, True), (1, False), (1, True)),
-        state,
+        None,
         None,
         "attend_near",
     )
+    weights, near = lax.optimization_barrier((weights, near))
+    weights_got = move(weights, 0, 1)
     context = attend(
         doc_length,
         queries,
         (own_far, peer_far),
         ((2, False), (2, True)),
-        state,
-        near,
+        (here, near),
+        blocks,
         "attend_far",
     )
     context = lax.all_to_all(context, "head", 0, 0, axis_index_groups=y_groups, tiled=True)

time: 276 us -> 235 us (0.85)
  the two profiles are of different devices: /device:TPU:0 before, /device:TPU:2 now
where the time goes in v3:
time: 235 us
  Pallas kernels  144 us (61%)
  blocking collectives  35.8 us (15%)
  waiting for transfers between devices  31.9 us (14%)
  starting transfers between devices  15.2 us (6%)
  local copies, waits for them, and re-layouts  6.18 us (3%)
    pallas_call x3, Pallas kernels, attend(): pl.pallas_call(functools.partial(attend_kernel, places, first, last), in_...  131 us
    ppermute x9, waiting for transfers between devices, move(): lax.ppermute(array, 'seq', [(i, (i // 2 + by) % 4 * 2 + (i % 2 ^ cross))...  31.9 us
    all_to_all x1, blocking collectives, body(): terms = lax.all_to_all(terms, 'head', 0, 0, tiled=True).astype(F32)  21.5 us
    all_to_all x1, blocking collectives, body(): lax.all_to_all(context, 'head', 0, 0, axis_index_groups=y_groups, tiled=T...  14.3 us
    ppermute x9, starting transfers between devices, move(): lax.ppermute(array, 'seq', [(i, (i // 2 + by) % 4 * 2 + (i % 2 ^ cross))...  10.6 us
    pallas_call x1, Pallas kernels, project(): pl.pallas_call(project_kernel, in_specs=[HBM] * 3, out_specs=(HBM, HBM),...  6.24 us
    unnamed x26, local copies, waits for them, and re-layouts  6.18 us
  transfers between devices with their start and end apart: 10, of which 6 were waited for; matrix products, arithmetic and copies ran while one was open for 0% of the time, Pallas kernels for 56%

profile of v3, /device:TPU:2, one launch (start us, length us, event | category | flops | bytes accessed | tf_op | source)
XLA Modules:
  0.0 234.8 jit_solution(15384392855526907303)
XLA Ops:
  0.0 6.2 %project.1 = (bf16[1040,256]{1,0:T(8,128)(2,1)}, bf16[1040,256]{1,0:T(8,128)(2,1)}) custom-call(bf16[1024,2048]{1,0:T(8,128)(2,1)} %x_ref.1, bf16[2048,256]{1,0:T(8,128)(2,1)} %ws_ref.1, bf16[2048,256]{1,0:T(8,128)(2,1)} %wv_ref.1), custom_call_target="tpu_custom_call" | custom-call | flops 2147483648 | bytes 7340032 | tf_op jit(solution)/shard_map/project/pallas_call | solution.py:109
  6.2 0.1 collective-permute-start
  6.3 2.1 collective-permute-done.refs_1_.after_ref
  8.5 0.0 copy-start.3
  8.5 0.8 copy-done.3
  9.3 2.4 %spread.1 = bf16[4,128,2048]{2,1,0:T(8,128)(2,1)} custom-call(bf16[256,2048]{1,0:T(8,128)(2,1)} %w_ref.1, bf16[1040,256]{1,0:T(8,128)(2,1)} %copy-done.3), custom_call_target="tpu_custom_call" | custom-call | tf_op jit(solution)/shard_map/spread/pallas_call | solution.py:142
  11.7 0.0 copy-start.10
  11.7 0.0 copy-start.5
  11.7 4.6 %all-to-all-start = ((bf16[4,128,2048]{2,1,0:T(8,128)(2,1)}), bf16[4,128,2048]{2,1,0:T(8,128)(2,1)S(1)}, u32[]{:S(2)}, u32[]{:S(2)}) async-start(bf16[4,128,2048]{2,1,0:T(8,128)(2,1)} %spread.1), calls=%async_computation | async-start | bytes 4194304 | tf_op jit(solution)/shard_map/all_to_all | solution.py:431
  16.3 0.0 copy-done.10
  16.3 3.5 %collective-permute-start.2 = (bf16[1040,256]{1,0:T(8,128)(2,1)S(1)}, bf16[1040,256]{1,0:T(8,128)(2,1)S(1)}, u32[]{:S(2)}, u32[]{:S(2)}) collective-permute-start(bf16[1040,256]{1,0:T(8,128)(2,1)S(1)} %copy-done.10), channel_id=1, source_target_pairs={{0,112},{16,96},{32,16},{48,0},{64,48},{80,32},{96,80},{112,64},{1... | collective-permute-start | bytes 1597448 | tf_op jit(solution)/shard_map/ppermute | solution.py:421
  19.8 0.0 copy-done.5
  19.8 0.0 collective-permute-start.1
  19.8 0.0 collective-permute-start.5
  19.8 3.5 %collective-permute-start.6 = (bf16[1040,256]{1,0:T(8,128)(2,1)S(1)}, bf16[1040,256]{1,0:T(8,128)(2,1)S(1)}, u32[]{:S(2)}, u32[]{:S(2)}) collective-permute-start(bf16[1040,256]{1,0:T(8,128)(2,1)S(1)} %copy-done.5), channel_id=1, source_target_pairs={{0,96},{16,112},{32,0},{48,16},{64,32},{80,48},{96,64},{112,80},{1... | collective-permute-start | bytes 1597448 | tf_op jit(solution)/shard_map/ppermute | solution.py:421
  24.0 7.5 %attend_here.1.refs_4_ = f32[2,1024,256]{2,1,0:T(8,128)} custom-call(s32[1]{0:T(128)S(6)} %copy.6.doc_ref, bf16[1040,256]{1,0:T(8,128)(2,1)} %get-tuple-element.12.refs_0_, bf16[1040,256]{1,0:T(8,128)(2,1)} %copy-done.3), custom_call_target="tpu_custom_call" | custom-call | flops 4294967296 | bytes 4194304 | tf_op jit(solution)/shard_map/attend_here/pallas_call | solution.py:336
  31.5 0.8 collective-permute-done.2.refs_5_.refs_9_
  32.3 0.0 copy-start.6
  32.3 3.7 %collective-permute-done.1.refs_2_.refs_6_ = bf16[1040,256]{1,0:T(8,128)(2,1)S(1)} collective-permute-done((bf16[1040,256]{1,0:T(8,128)(2,1)S(1)}, bf16[1040,256]{1,0:T(8,128)(2,1)S(1)}, u32[]{:S(2)}, u32[]{:S(2)}) %collective-permute-start.1) | collective-permute-done | bytes 532512 | tf_op jit(solution)/shard_map/ppermute | solution.py:421
  36.0 10.8 %collective-permute-done.5.refs_3_.refs_7_ = bf16[1040,256]{1,0:T(8,128)(2,1)S(1)} collective-permute-done((bf16[1040,256]{1,0:T(8,128)(2,1)S(1)}, bf16[1040,256]{1,0:T(8,128)(2,1)S(1)}, u32[]{:S(2)}, u32[]{:S(2)}) %collective-permute-start.5) | collective-permute-done | bytes 532512 | tf_op jit(solution)/shard_map/ppermute | solution.py:421
  46.8 0.0 collective-permute-done.6.refs_4_.refs_8_
  46.8 0.0 copy-done.6
  46.8 0.0 copy-done.7
  46.8 0.8 copy-done.8
  47.6 0.8 copy-done.9
  48.4 13.0 %attend_near.1.refs_5_ = f32[2,1024,256]{2,1,0:T(8,128)} custom-call(s32[1]{0:T(128)S(6)} %copy.6.doc_ref, bf16[1040,256]{1,0:T(8,128)(2,1)} %get-tuple-element.12.refs_0_, bf16[1040,256]{1,0:T(8,128)(2,1)} %copy-done.3, bf16[1040,256]{1,0:T(8,128)(2,1)} %copy-done.7, bf16[1040,256]{1,0:T(8,128)(2,1)} %copy-done.8, bf16[1040,256]{1,0:T(8,128)(2,1)} %copy-done.9, ...), custom_call_target="tpu_custom_call" | custom-call | flops 8589934592 | bytes 4194304 | tf_op jit(solution)/shard_map/attend_near/pallas_call | solution.py:336
  61.5 0.0 all-to-all-done.w_ref
  61.5 0.0 copy-start
  61.5 0.2 collective-permute-start.8
  61.7 0.0 collective-permute-start.3
  61.7 3.2 %collective-permute-start.4 = (bf16[1040,256]{1,0:T(8,128)(2,1)}, bf16[1040,256]{1,0:T(8,128)(2,1)S(1)}, u32[]{:S(2)}, u32[]{:S(2)}) collective-permute-start(bf16[1040,256]{1,0:T(8,128)(2,1)} %copy-done.6), channel_id=1, source_target_pairs={{0,96},{16,112},{32,0},{48,16},{64,32},{80,48},{96,64},{112,80},{1... | collective-permute-start | bytes 1597448 | tf_op jit(solution)/shard_map/ppermute | solution.py:421
  65.0 12.5 %collective-permute-done.3.refs_2_ = bf16[1040,256]{1,0:T(8,128)(2,1)S(1)} collective-permute-done((bf16[1040,256]{1,0:T(8,128)(2,1)}, bf16[1040,256]{1,0:T(8,128)(2,1)S(1)}, u32[]{:S(2)}, u32[]{:S(2)}) %collective-permute-start.3) | collective-permute-done | bytes 532512 | tf_op jit(solution)/shard_map/ppermute | solution.py:421
  77.5 0.0 collective-permute-done.4.refs_3_
  77.5 0.8 copy-done.11
  78.3 0.8 copy-done.12
  79.1 110.6 %attend_far.1 = bf16[4,2,256,128]{3,2,1,0:T(8,128)(2,1)} custom-call(s32[1]{0:T(128)S(6)} %copy.6.doc_ref, bf16[1040,256]{1,0:T(8,128)(2,1)} %get-tuple-element.12.refs_0_, bf16[1040,256]{1,0:T(8,128)(2,1)} %copy-done.3, bf16[1040,256]{1,0:T(8,128)(2,1)} %copy-done.11, bf16[1040,256]{1,0:T(8,128)(2,1)} %copy-done.12, f32[2,1024,256]{2,1,0:T(8,128)} %attend_here.1.refs_4_, ...), custom_call_target="tpu_custom_call" | custom-call | flops 4294967296 | bytes 4194304 | tf_op jit(solution)/shard_map/attend_far/pallas_call | solution.py:336
  189.7 0.0 copy-done
  189.8 14.3 %all_to_all.15.ctx_ref = bf16[4,2,256,128]{3,2,1,0:T(8,128)(2,1)S(1)} all-to-all(bf16[4,2,256,128]{3,2,1,0:T(8,128)(2,1)} %attend_far.1), channel_id=1, replica_groups={{0,2,4,6},{8,10,12,14},{1,3,5,7},{9,11,13,15},{16,18,20,22},{24,26,28,3..., dimensions={0} | all-to-all | bytes 1048576 | tf_op jit(solution)/shard_map/all_to_all | solution.py:460
  204.1 0.0 collective-permute-start.7
  204.1 1.9 collective-permute-done.7.got_ref
  206.0 0.0 collective-permute-done.8.w_got_ref
  206.0 0.0 copy-done.2
  206.0 0.8 copy-done.4
  206.8 1.3 copy-done.1
  208.1 4.0 %output.1 = bf16[8,256,256]{2,1,0:T(8,128)(2,1)} custom-call(bf16[4,2,256,128]{3,2,1,0:T(8,128)(2,1)} %copy-done.2, bf16[4,2,256,128]{3,2,1,0:T(8,128)(2,1)} %copy-done.4, bf16[4,128,2048]{2,1,0:T(8,128)(2,1)} %copy-done, bf16[4,128,2048]{2,1,0:T(8,128)(2,1)} %copy-done.1), custom_call_target="tpu_custom_call" | custom-call | flops 1073741824 | bytes 6291456 | tf_op jit(solution)/shard_map/output/pallas_call | solution.py:399
  212.1 21.5 %all_to_all.16 = bf16[8,256,256]{2,1,0:T(8,128)(2,1)S(1)} all-to-all(bf16[8,256,256]{2,1,0:T(8,128)(2,1)} %output.1), channel_id=1, replica_groups=mesh['seq'=8,'head'=8,'batch'=2] {'head'}, dimensions={0} | all-to-all | bytes 2097152 | tf_op jit(solution)/shard_map/all_to_all | solution.py:462
  233.5 0.2 convert_element_type.6
  233.7 0.9 fusion
  (8 shorter events, 0.0 us)
Async XLA Ops:
  6.2 2.2 collective-permute-start
  8.5 0.8 copy-start.3
  11.7 4.6 %copy-start.10 = (bf16[1040,256]{1,0:T(8,128)(2,1)S(1)}, bf16[1040,256]{1,0:T(8,128)(2,1)}, u32[]{:S(2)}) copy-start(bf16[1040,256]{1,0:T(8,128)(2,1)} %get-tuple-element.13) | copy-start | bytes 1597444
  11.7 8.1 %copy-start.5 = (bf16[1040,256]{1,0:T(8,128)(2,1)S(1)}, bf16[1040,256]{1,0:T(8,128)(2,1)}, u32[]{:S(2)}) copy-start(bf16[1040,256]{1,0:T(8,128)(2,1)} %get-tuple-element.12.refs_0_) | copy-start | bytes 1597444
  11.7 49.8 %all-to-all-start = ((bf16[4,128,2048]{2,1,0:T(8,128)(2,1)}), bf16[4,128,2048]{2,1,0:T(8,128)(2,1)S(1)}, u32[]{:S(2)}, u32[]{:S(2)}) async-start(bf16[4,128,2048]{2,1,0:T(8,128)(2,1)} %spread.1), calls=%async_computation | async-start | bytes 4194304 | tf_op jit(solution)/shard_map/all_to_all | solution.py:431
  16.3 16.0 %collective-permute-start.2 = (bf16[1040,256]{1,0:T(8,128)(2,1)S(1)}, bf16[1040,256]{1,0:T(8,128)(2,1)S(1)}, u32[]{:S(2)}, u32[]{:S(2)}) collective-permute-start(bf16[1040,256]{1,0:T(8,128)(2,1)S(1)} %copy-done.10), channel_id=1, source_target_pairs={{0,112},{16,96},{32,16},{48,0},{64,48},{80,32},{96,80},{112,64},{1... | collective-permute-start | bytes 1597448 | tf_op jit(solution)/shard_map/ppermute | solution.py:421
  19.8 16.2 %collective-permute-start.1 = (bf16[1040,256]{1,0:T(8,128)(2,1)S(1)}, bf16[1040,256]{1,0:T(8,128)(2,1)S(1)}, u32[]{:S(2)}, u32[]{:S(2)}) collective-permute-start(bf16[1040,256]{1,0:T(8,128)(2,1)S(1)} %copy-done.5), channel_id=1, source_target_pairs={{0,32},{16,48},{32,64},{48,80},{64,96},{80,112},{96,0},{112,16},{1... | collective-permute-start | bytes 1597448 | tf_op jit(solution)/shard_map/ppermute | solution.py:421
  19.8 27.0 %collective-permute-start.5 = (bf16[1040,256]{1,0:T(8,128)(2,1)S(1)}, bf16[1040,256]{1,0:T(8,128)(2,1)S(1)}, u32[]{:S(2)}, u32[]{:S(2)}) collective-permute-start(bf16[1040,256]{1,0:T(8,128)(2,1)S(1)} %copy-done.10), channel_id=1, source_target_pairs={{0,48},{16,32},{32,80},{48,64},{64,112},{80,96},{96,16},{112,0},{1... | collective-permute-start | bytes 1597448 | tf_op jit(solution)/shard_map/ppermute | solution.py:421
  19.8 27.0 %collective-permute-start.6 = (bf16[1040,256]{1,0:T(8,128)(2,1)S(1)}, bf16[1040,256]{1,0:T(8,128)(2,1)S(1)}, u32[]{:S(2)}, u32[]{:S(2)}) collective-permute-start(bf16[1040,256]{1,0:T(8,128)(2,1)S(1)} %copy-done.5), channel_id=1, source_target_pairs={{0,96},{16,112},{32,0},{48,16},{64,32},{80,48},{96,64},{112,80},{1... | collective-permute-start | bytes 1597448 | tf_op jit(solution)/shard_map/ppermute | solution.py:421
  32.3 14.5 %copy-start.6 = (bf16[1040,256]{1,0:T(8,128)(2,1)}, bf16[1040,256]{1,0:T(8,128)(2,1)S(1)}, u32[]{:S(2)}) copy-start(bf16[1040,256]{1,0:T(8,128)(2,1)S(1)} %collective-permute-done.2.refs_5_.refs_9_) | copy-start | bytes 1597444
  36.0 10.8 %copy-start.7 = (bf16[1040,256]{1,0:T(8,128)(2,1)}, bf16[1040,256]{1,0:T(8,128)(2,1)S(1)}, u32[]{:S(2)}) copy-start(bf16[1040,256]{1,0:T(8,128)(2,1)S(1)} %collective-permute-done.1.refs_2_.refs_6_) | copy-start | bytes 1597444
  46.8 0.9 copy-start.8
  47.6 0.8 copy-start.9
  61.5 128.3 %copy-start = (bf16[4,128,2048]{2,1,0:T(8,128)(2,1)}, bf16[4,128,2048]{2,1,0:T(8,128)(2,1)S(1)}, u32[]{:S(2)}) copy-start(bf16[4,128,2048]{2,1,0:T(8,128)(2,1)S(1)} %all-to-all-done.w_ref) | copy-start | bytes 6291460
  61.5 144.5 %collective-permute-start.8 = (bf16[4,128,2048]{2,1,0:T(8,128)(2,1)S(1)}, bf16[4,128,2048]{2,1,0:T(8,128)(2,1)S(1)}, u32[]{:S(2)}, u32[]{:S(2)}) collective-permute-start(bf16[4,128,2048]{2,1,0:T(8,128)(2,1)S(1)} %all-to-all-done.w_ref), channel_id=1, source_target_pairs={{0,16},{16,0},{32,48},{48,32},{64,80},{80,64},{96,112},{112,96},{1... | collective-permute-start | bytes 6291464 | tf_op jit(solution)/shard_map/ppermute | solution.py:421
  61.7 15.8 %collective-permute-start.3 = (bf16[1040,256]{1,0:T(8,128)(2,1)}, bf16[1040,256]{1,0:T(8,128)(2,1)S(1)}, u32[]{:S(2)}, u32[]{:S(2)}) collective-permute-start(bf16[1040,256]{1,0:T(8,128)(2,1)} %copy-done.7), channel_id=1, source_target_pairs={{0,32},{16,48},{32,64},{48,80},{64,96},{80,112},{96,0},{112,16},{1... | collective-permute-start | bytes 1597448 | tf_op jit(solution)/shard_map/ppermute | solution.py:421
  61.7 15.8 %collective-permute-start.4 = (bf16[1040,256]{1,0:T(8,128)(2,1)}, bf16[1040,256]{1,0:T(8,128)(2,1)S(1)}, u32[]{:S(2)}, u32[]{:S(2)}) collective-permute-start(bf16[1040,256]{1,0:T(8,128)(2,1)} %copy-done.6), channel_id=1, source_target_pairs={{0,96},{16,112},{32,0},{48,16},{64,32},{80,48},{96,64},{112,80},{1... | collective-permute-start | bytes 1597448 | tf_op jit(solution)/shard_map/ppermute | solution.py:421
  77.5 0.8 copy-start.11
  78.3 0.8 copy-start.12
  204.1 1.9 copy-start.2
  204.1 1.9 collective-permute-start.7
  206.0 0.8 copy-start.4
  206.8 1.3 copy-start.1
